TPU v7x, 256 devices: a whole 4x4x8 slice. The times are simulated.
256 devices in a mesh: section: 2 (over y_lo), ep: 64 (over z, x, core), tp: 2 (over y_hi).
Axes of the slice: x: 4, y: 4 (y_hi: 2, y_lo: 2; y = y_hi * 2 + y_lo), z: 8, core: 2. Of those that a mesh axis runs over, the one named last changes fastest.
Arguments:
- prompt_latent: bfloat16 [8192, 576], P('ep'), may hold values from -6 to 6
- prompt_dest: int32 [8192, 1], P('ep'), may hold values from 0 to 63; in each aligned block of 128 rows (0 to 127, 128 to 255, ...) at most 4 rows name the same one
- prompt_slot: int32 [8192], P('ep'), may hold values from 0 to 7
- old_cache: bfloat16 [512, 128, 576], P('ep'), may hold values from -6 to 6
- cache_len: int32 [512], P('ep'), may hold values from 1 to 128, 32768 in all
- new_latent: bfloat16 [512, 4, 576], P('ep'), may hold values from -6 to 6
- dec_query: bfloat16 [512, 4, 128, 576], P('ep', None, ('section', 'tp')), may hold values from -48 to 48
- dec_states: bfloat16 [512, 4, 7168], P('ep', None, ('section', 'tp')), may hold values from -6 to 6
- moe_gain: float32 [7168], P(('section', 'tp')), may hold values from 0.1 to 1.9
- expert_ids: int32 [512, 4, 8], P('ep'), may hold values from 0 to 63, all different within a row; in each aligned block of 32 rows (0 to 31, 32 to 63, ..., all dimensions but the last counted through in order) at most 8 rows name the same one
- route_weight: int32 [512, 4, 8], P('ep'), may hold values from 1 to 1024
- w_gate: bfloat16 [64, 7168, 1024], P('ep', None, ('section', 'tp')), may hold values from -0.0625 to 0.0625
- w_up: bfloat16 [64, 7168, 1024], P('ep', None, ('section', 'tp')), may hold values from -0.0625 to 0.0625
- w_down: bfloat16 [64, 1024, 7168], P('ep', ('section', 'tp')), may hold values from -0.1875 to 0.1875
Outputs:
- attn_out: bfloat16 [512, 4, 128, 512], P('ep', None, ('section', 'tp'))
- moe_out: bfloat16 [512, 4, 7168], P('ep', None, ('section', 'tp'))
Inputs may be any that keep to these rules, and one draw needn't show every extreme that they name: `prompt_dest`: the prompt tokens of one index of ep name one owner at most 4 times, and some owner exactly that often. `expert_ids`: each token names 8 different experts; the tokens of one index of ep name one expert at most 8 times, and some expert exactly that often.
All inputs are finite; a program needn't handle non-finite values. No bound on the sum of `cache_len` on one device may be relied on, other than what follows from the above.
Results may differ from a plain program's by a relative error of at most 0.015.
Values may be sent and summed in bfloat16 or wider, within the bound.
No kernel may reach another device: no remote copies, remote signals or barrier semaphores. Data moves between devices by JAX's collectives and lax.ppermute only.
A program may use at most 128 MiB of HBM per device.

v0:
```python
import jax
import jax.numpy as jnp
from jax import lax
from jax.experimental import pallas as pl
from jax.experimental.pallas import tpu as pltpu
from jax.sharding import PartitionSpec as P

LAT = 512
EPS = 1e-06
SCORE_SCALE = 192.0 ** (-0.5)
NY = 4
ORDER = (0, 1, 3, 2)
E_CAP = 8
PEER_CAP = 4
CHUNKS = 2
SCOPED = 16 * 2**20
GROUP = ("section", "tp")


def group_of_y(y):
    return (y % 2) * 2 + (y // 2) % 2


def y_perm(k):
    return [(group_of_y(y), group_of_y((y + k) % NY)) for y in range(NY)]


def over_y(v, k):
    return lax.ppermute(v, GROUP, y_perm(k % NY)) if k % NY else v


def other_core(v):
    return lax.ppermute(v, "ep", [(i, i ^ 1) for i in range(lax.axis_size("ep"))])


def chips_exchange(v):
    n = lax.axis_size("ep")
    groups = [[i for i in range(n) if i % 2 == core] for core in range(2)]
    return lax.all_to_all(
        v, "ep", split_axis=0, concat_axis=0, tiled=True, axis_index_groups=groups
    )


def dot(a, b):
    return jnp.dot(a, b, preferred_element_type=jnp.float32)


def slots(names, half_tokens, cap):
    tokens = names.shape[1]
    i = jnp.arange(tokens, dtype=jnp.int32)
    own = i[:, None] // half_tokens == i[None, :] // half_tokens
    earlier = ((i[:, None] < i[None, :]) & own).astype(jnp.bfloat16)
    rank = dot(names.astype(jnp.bfloat16), earlier)
    side = i[None, :] // half_tokens == jnp.arange(2, dtype=jnp.int32)[:, None]
    slot = jnp.where(names[:, None, :] & side[None], rank[:, None, :], -1.0)
    return slot[:, :, None, :] == jnp.arange(cap, dtype=jnp.float32)[None, None, :, None]


def prompt_rows(prompt_latent, prompt_dest, prompt_slot, chips, core):
    ptok_dev, width = prompt_latent.shape
    tags = jnp.stack([prompt_slot + 1, prompt_dest[:, 0]], axis=1).astype(jnp.bfloat16)
    spare = jnp.zeros((ptok_dev, -(width + 2) % 128), jnp.bfloat16)
    tagged = jnp.concatenate([prompt_latent, tags, spare], axis=1)
    tagged = jnp.concatenate([tagged, other_core(tagged)], axis=0)
    dest = tagged[:, width + 1].astype(jnp.int32)
    owners = 2 * jnp.arange(chips, dtype=jnp.int32) + core
    chosen = slots(dest[None, :] == owners[:, None], ptok_dev, PEER_CAP)
    pick = chosen.astype(jnp.bfloat16).reshape(chips * 2 * PEER_CAP, 2 * ptok_dev)
    return dot(pick, tagged).astype(jnp.bfloat16)


WHOLE = pl.BlockSpec(memory_space=pltpu.VMEM)


def near_kernel(own, below, above, *refs):
    weights, out = refs[:-1], refs[-1]
    cols = weights[0].shape[1]
    gate, up = 0.0, 0.0
    for rows, gate_w, up_w in zip((own, below, above), weights[0::2], weights[1::2]):
        gate = gate + dot(rows[...], gate_w[...])
        up = up + dot(rows[...], up_w[...])
    out[:, :cols] = gate
    out[:, cols:] = up


def near_sums(own, below, above, weights):
    n, depth = own.shape
    cols = weights[0].shape[1]
    return pl.pallas_call(
        near_kernel,
        out_shape=jax.ShapeDtypeStruct((n, 2 * cols), jnp.float32),
        in_specs=[WHOLE] * (3 + len(weights)),
        out_specs=WHOLE,
        compiler_params=pltpu.CompilerParams(vmem_limit_bytes=SCOPED),
        cost_estimate=pl.CostEstimate(
            flops=12 * n * depth * cols, bytes_accessed=12 * depth * cols, transcendentals=0
        ),
        name="near_sums",
    )(own, below, above, *weights)


def hidden_kernel(low, high, sums, gate_w, up_w, out):
    n, cols = out.shape
    mid = n // 2
    for rows, first in ((low, 0), (high, mid)):
        at = slice(first, first + mid)
        gate = sums[at, :cols] + dot(rows[...], gate_w[...])
        up = sums[at, cols:] + dot(rows[...], up_w[...])
        out[at, :] = (gate / (1.0 + jnp.exp(-gate)) * up).astype(out.dtype)


def hidden_units(low, high, sums, gate_w, up_w):
    mid, depth = low.shape
    cols = gate_w.shape[1]
    return pl.pallas_call(
        hidden_kernel,
        out_shape=jax.ShapeDtypeStruct((2 * mid, cols), jnp.bfloat16),
        in_specs=[WHOLE] * 5,
        out_specs=WHOLE,
        compiler_params=pltpu.CompilerParams(vmem_limit_bytes=SCOPED),
        cost_estimate=pl.CostEstimate(
            flops=8 * mid * depth * cols,
            bytes_accessed=4 * depth * cols,
            transcendentals=2 * mid * cols,
        ),
        name="hidden_units",
    )(low, high, sums, gate_w, up_w)


def down_kernel(n_hidden, n_downs, *refs):
    hidden, downs = refs[:n_hidden], refs[n_hidden : n_hidden + n_downs]
    out = refs[-1]
    depth, cols = downs[0].shape
    tile = 256 if cols % 256 == 0 else 128

    @pl.loop(0, cols // tile)
    def _(step):
        at = pl.ds(pl.multiple_of(step * tile, tile), tile)
        total = 0.0
        for k, w in enumerate(downs[:-2]):
            total = total + dot(hidden[k][...], w[:depth, at])
        rows = 0
        for w in downs[-2:]:
            total = total + dot(hidden[-1][:, rows : rows + w.shape[0]], w[:, at])
            rows += w.shape[0]
        out[:, at] = total.astype(out.dtype)

    if len(refs) > n_hidden + n_downs + 1:
        out[:, cols:] = refs[-2][...]


def down_product(hidden, downs, rider=None):
    n, depth = hidden[0].shape
    cols = downs[0].shape[1]
    more = [] if rider is None else [rider]
    return pl.pallas_call(
        lambda *refs: down_kernel(len(hidden), len(downs), *refs),
        out_shape=jax.ShapeDtypeStruct(
            (n, cols + sum(v.shape[1] for v in more)), jnp.bfloat16
        ),
        in_specs=[WHOLE] * (len(hidden) + len(downs) + len(more)),
        out_specs=WHOLE,
        compiler_params=pltpu.CompilerParams(vmem_limit_bytes=SCOPED),
        cost_estimate=pl.CostEstimate(
            flops=2 * n * depth * cols * len(hidden),
            bytes_accessed=2 * depth * cols * len(hidden),
            transcendentals=0,
        ),
        name="down_product",
    )(*hidden, *downs, *more)


def attention(got, old_cache, cache_len, new_latent, dec_query):
    seq_dev, steps, heads_dev, width = dec_query.shape
    got_rows = got[:, :width]
    got_tags = got[:, width].astype(jnp.float32) - 1.0
    queries = dec_query.reshape(seq_dev, steps * heads_dev, width)
    old_scores = (
        jnp.einsum("sqw,skw->sqk", queries, old_cache, preferred_element_type=jnp.float32)
        * SCORE_SCALE
    )
    got_scores = (
        jnp.einsum("sqw,kw->sqk", queries, got_rows, preferred_element_type=jnp.float32)
        * SCORE_SCALE
    )
    new_scores = (
        jnp.einsum("sqw,skw->sqk", queries, new_latent, preferred_element_type=jnp.float32)
        * SCORE_SCALE
    )
    old_live = (
        jnp.arange(old_cache.shape[1], dtype=jnp.int32)[None, None, :] < cache_len[:, None, None]
    )
    got_live = got_tags[None, None, :] == jnp.arange(seq_dev, dtype=jnp.float32)[:, None, None]
    query_step = jnp.arange(steps * heads_dev, dtype=jnp.int32) // heads_dev
    new_live = jnp.arange(steps, dtype=jnp.int32)[None, None, :] <= query_step[None, :, None]
    old_scores = jnp.where(old_live, old_scores, -jnp.inf)
    got_scores = jnp.where(got_live, got_scores, -jnp.inf)
    new_scores = jnp.where(new_live, new_scores, -jnp.inf)
    top = jnp.maximum(
        jnp.maximum(jnp.max(old_scores, axis=2), jnp.max(got_scores, axis=2)),
        jnp.max(new_scores, axis=2),
    )[:, :, None]
    old_weights = jnp.exp(old_scores - top)
    got_weights = jnp.exp(got_scores - top)
    new_weights = jnp.exp(new_scores - top)
    total = (
        jnp.sum(old_weights, axis=2) + jnp.sum(got_weights, axis=2) + jnp.sum(new_weights, axis=2)
    )
    summed = jnp.einsum(
        "mpl,mlf->mpf",
        old_weights.astype(jnp.bfloat16),
        old_cache[:, :, :LAT],
        preferred_element_type=jnp.float32,
    )
    summed = summed + jnp.einsum(
        "sqk,kv->sqv",
        got_weights.astype(jnp.bfloat16),
        got_rows[:, :LAT],
        preferred_element_type=jnp.float32,
    )
    summed = summed + jnp.einsum(
        "mpl,mlf->mpf",
        new_weights.astype(jnp.bfloat16),
        new_latent[:, :, :LAT],
        preferred_element_type=jnp.float32,
    )
    return (summed / total[:, :, None]).astype(jnp.bfloat16).reshape(seq_dev, steps, heads_dev, LAT)


def experts(dec_states, moe_gain, expert_ids, route_weight, w_gate, w_up, w_down, prompts, attend):
    seq_dev, steps, d_part = dec_states.shape
    tok = seq_dev * steps
    topk = expert_ids.shape[-1]
    chips = lax.axis_size("ep") // 2
    core = lax.axis_index("ep") % 2
    y = 2 * lax.axis_index("tp") + lax.axis_index("section")

    def part_of(k):
        return group_of_y((y + k) % NY)

    wide = dec_states.reshape(tok, d_part).astype(jnp.float32)
    squares = jnp.sum(wide * wide, axis=1)
    square_sum = squares
    for k in range(1, NY):
        square_sum = square_sum + over_y(squares, k)
    scale = lax.rsqrt(square_sum / (d_part * NY) + EPS)[:, None]
    normed = (wide * scale * moe_gain).astype(jnp.bfloat16)
    kept, upward, downward, across = [
        lax.dynamic_slice_in_dim(w_down[0], part_of(k) * d_part, d_part, axis=1) for k in ORDER
    ]
    units = across.shape[0]
    upward = jnp.concatenate([upward, across[: units // 2]], axis=0)
    downward = jnp.concatenate([downward, across[units // 2 :]], axis=0)
    upward, downward = over_y(upward, 1), over_y(downward, -1)
    downs = [kept, upward, downward, over_y(upward[units:], 1), over_y(downward[units:], -1)]
    meta = jnp.concatenate(
        [expert_ids.reshape(tok, topk), route_weight.reshape(tok, topk)], axis=1
    ).astype(jnp.float32)
    meta = jnp.concatenate([meta, other_core(meta)], axis=0)
    normed = jnp.concatenate([normed, other_core(normed)], axis=0)
    ids = meta[:, :topk].astype(jnp.int32)
    here = 2 * jnp.arange(chips, dtype=jnp.int32) + core
    named = ids.T[:, None, :] == here[None, :, None]
    chosen = slots(jnp.any(named, axis=0), tok, E_CAP)
    half = E_CAP // CHUNKS
    n = chips * 2 * half
    chosen = [chosen[:, :, c * half : (c + 1) * half] for c in range(CHUNKS)]
    picks = [v.astype(jnp.bfloat16).reshape(n, 2 * tok) for v in chosen]

    def exchange(v):
        return chips_exchange(v.reshape(chips, 2 * half, -1)).reshape(n, -1)

    sends = [dot(pick, normed).astype(jnp.bfloat16) for pick in picks]
    first = exchange(sends[0])
    first, second, gate_w, up_w = lax.optimization_barrier(
        (first, sends[1], w_gate[0], w_up[0])
    )
    blocks = [
        lax.dynamic_slice_in_dim(source, part_of(k) * d_part, d_part, axis=0)
        for k in (0, NY - 1, 1, 2)
        for source in (gate_w, up_w)
    ]
    arrived = [first, exchange(second)]

    def neighbours(rows):
        return over_y(rows, 1), over_y(rows, -1)

    near = [neighbours(rows) for rows in arrived]

    weight = meta[:, topk : 2 * topk]
    share = weight / jnp.sum(weight, axis=1, keepdims=True)
    gives = jnp.sum(jnp.where(named, share.T[:, None, :], 0.0), axis=0)
    mixes = []
    for v in chosen:
        mix = jnp.where(v, gives[:, None, None, :], 0.0).reshape(n, 2 * tok)
        high = lax.reduce_precision(mix, 8, 7)
        mixes.append([high.astype(jnp.bfloat16), (mix - high).astype(jnp.bfloat16)])
    mixed = 0.0
    contract = (((0,), (0,)), ((), ()))
    for c in range(CHUNKS):
        below, above = near[c]
        if c == 0:
            below, above, downs, blocks = lax.optimization_barrier((below, above, downs, blocks))
        mid = n // 2
        low, high = over_y(below[:mid], 1), over_y(above[mid:], -1)
        sums = near_sums(arrived[c], below, above, blocks[:6])
        hidden = hidden_units(low, high, sums, *blocks[6:])
        hidden = [over_y(hidden, k) for k in ORDER]
        out = down_product(hidden, downs, prompts if c == 0 else None)
        if c == 0:
            out, *near[1] = lax.optimization_barrier((out, *near[1]))
        back = exchange(out)
        if c == 0:
            attn_out = attend(back[:, d_part:])
        else:
            back, attn_out, mixed, mixes = lax.optimization_barrier((back, attn_out, mixed, mixes))
        for part in mixes[c]:
            mixed = mixed + lax.dot_general(
                part, back[:, :d_part], contract, preferred_element_type=jnp.float32
            )
    mixed = mixed[:tok] + other_core(mixed[tok:].astype(jnp.bfloat16)).astype(jnp.float32)
    return mixed.astype(jnp.bfloat16).reshape(seq_dev, steps, d_part), attn_out


def body(
    prompt_latent,
    prompt_dest,
    prompt_slot,
    old_cache,
    cache_len,
    new_latent,
    dec_query,
    dec_states,
    moe_gain,
    expert_ids,
    route_weight,
    w_gate,
    w_up,
    w_down,
):
    ep_index, n_ep = lax.axis_index("ep"), lax.axis_size("ep")
    prompts = prompt_rows(prompt_latent, prompt_dest, prompt_slot, n_ep // 2, ep_index % 2)

    def attend(got):
        return attention(got, old_cache, cache_len, new_latent, dec_query)

    moe_out, attn_out = experts(
        dec_states, moe_gain, expert_ids, route_weight, w_gate, w_up, w_down, prompts, attend
    )
    return (attn_out, moe_out)


def solution(mesh):
    placed = (
        P("ep", None),
        P("ep", None),
        P("ep"),
        P("ep", None, None),
        P("ep"),
        P("ep", None, None),
        P("ep", None, GROUP, None),
        P("ep", None, GROUP),
        P(GROUP),
        P("ep", None, None),
        P("ep", None, None),
        P("ep", None, GROUP),
        P("ep", None, GROUP),
        P("ep", GROUP, None),
    )
    return jax.shard_map(
        body,
        mesh=mesh,
        in_specs=placed,
        out_specs=(P("ep", None, GROUP, None), P("ep", None, GROUP)),
        check_vma=False,
    )
```

profile of v0, /device:TPU:1, one launch (start us, length us, event | category | flops | bytes accessed | tf_op | source)
XLA Modules:
  0.0 217.9 jit_solution(16586323368056117082)
XLA Ops:
  1.9 3.6 %collective-permute-start.3 = (f32[32]{0:T(128)S(1)}, f32[32]{0:T(128)S(1)}, u32[]{:S(2)}, u32[]{:S(2)}) collective-permute-start(f32[32]{0:T(128)S(1)} %reduce_sum.57), channel_id=1, source_target_pairs={{0,129},{128,0},{1,128},{129,1},{2,131},{130,2},{3,130},{131,3},{4... | collective-permute-start | bytes 392 | tf_op jit(solution)/shard_map/ppermute | solution.py:29
  16.6 11.2 %all-to-all-start = ((bf16[32,8,1792]{2,1,0:T(8,128)(2,1)}), bf16[32,8,1792]{2,1,0:T(8,128)(2,1)}, u32[]{:S(2)}, u32[]{:S(2)}) async-start(bf16[32,8,1792]{2,1,0:T(8,128)(2,1)} %fusion), calls=%async_computation | async-start | bytes 1835008 | tf_op jit(solution)/shard_map/all_to_all | solution.py:39
  29.2 2.9 %dynamic-slice_bitcast_fusion = (bf16[256,1792]{1,0:T(8,128)(2,1)S(1)}, bf16[256,1792]{1,0:T(8,128)(2,1)S(1)}, bf16[256,1792]{1,0:T(8,128)(2,1)}) fusion(bf16[1,256,7168]{2,1,0:T(8,128)(2,1)} %param.27, s32[]{:T(128)S(6)} %select_n.258, s32[]{:T(128)S(6)} %select_n.248, s32[]{:T(128)S(6)} %select_n.243), kind=kLoop, calls=%fused_computation.22 | loop fusion | bytes 5505036 | tf_op jit(solution)/shard_map/dynamic_slice | solution.py:249
  34.5 2.7 %collective-permute-start.8 = (bf16[384,1792]{1,0:T(8,128)(2,1)}, bf16[384,1792]{1,0:T(8,128)(2,1)}, u32[]{:S(2)}, u32[]{:S(2)}) collective-permute-start(bf16[384,1792]{1,0:T(8,128)(2,1)} %pad_maximum_fusion.1), channel_id=1, source_target_pairs={{0,129},{128,0},{1,128},{129,1},{2,131},{130,2},{3,130},{131,3},{4... | collective-permute-start | bytes 4128776 | tf_op jit(solution)/shard_map/ppermute | solution.py:29
  38.4 13.9 %all-to-all-done = bf16[32,8,1792]{2,1,0:T(8,128)(2,1)} async-done(((bf16[32,8,1792]{2,1,0:T(8,128)(2,1)}), bf16[32,8,1792]{2,1,0:T(8,128)(2,1)}, u32[]{:S(2)}, u32[]{:S(2)}) %all-to-all-start) | async-done | bytes 917536 | tf_op jit(solution)/shard_map/all_to_all | solution.py:39
  52.4 5.4 %all-to-all-start.1 = ((bf16[32,8,1792]{2,1,0:T(8,128)(2,1)}), bf16[32,8,1792]{2,1,0:T(8,128)(2,1)}, u32[]{:S(2)}, u32[]{:S(2)}) async-start(bf16[32,8,1792]{2,1,0:T(8,128)(2,1)} %bitcast.69), calls=%async_computation.1 | async-start | bytes 1835008 | tf_op jit(solution)/shard_map/all_to_all | solution.py:39
  60.6 2.7 %collective-permute-start.6 = (bf16[256,1792]{1,0:T(8,128)(2,1)}, bf16[256,1792]{1,0:T(8,128)(2,1)S(1)}, u32[]{:S(2)}, u32[]{:S(2)}) collective-permute-start(bf16[256,1792]{1,0:T(8,128)(2,1)} %bitcast.5.own), channel_id=1, source_target_pairs={{0,129},{128,0},{1,128},{129,1},{2,131},{130,2},{3,130},{131,3},{4... | collective-permute-start | bytes 2752520 | tf_op jit(solution)/shard_map/ppermute | solution.py:29
  63.3 2.9 %collective-permute-done.7.refs_5_ = bf16[384,1792]{1,0:T(8,128)(2,1)S(1)} collective-permute-done((bf16[384,1792]{1,0:T(8,128)(2,1)}, bf16[384,1792]{1,0:T(8,128)(2,1)S(1)}, u32[]{:S(2)}, u32[]{:S(2)}) %collective-permute-start.7) | collective-permute-done | bytes 1376288 | tf_op jit(solution)/shard_map/ppermute | solution.py:29
  67.7 3.2 %collective-permute-start.10 = (bf16[128,1792]{1,0:T(8,128)(2,1)S(1)}, bf16[128,1792]{1,0:T(8,128)(2,1)S(1)}, u32[]{:S(2)}, u32[]{:S(2)}) collective-permute-start(bf16[128,1792]{1,0:T(8,128)(2,1)S(1)} %slice.103), channel_id=1, source_target_pairs={{0,129},{128,0},{1,128},{129,1},{2,131},{130,2},{3,130},{131,3},{4... | collective-permute-start | bytes 1376264 | tf_op jit(solution)/shard_map/ppermute | solution.py:29
  71.2 5.5 %constant_dynamic-slice_fusion = (bf16[1792,256]{1,0:T(8,128)(2,1)}, bf16[1792,256]{1,0:T(8,128)(2,1)S(1)}, bf16[1792,256]{1,0:T(8,128)(2,1)S(1)}, bf16[1792,256...) fusion(bf16[7168,256]{1,0:T(8,128)(2,1)} %bitcast.70, ...), kind=kLoop, calls=%fused_computation.100 | loop fusion | bytes 14680080 | tf_op jit(solution)/shard_map/dynamic_slice | solution.py:279
  76.7 18.9 %collective-permute-done.9.refs_7_ = bf16[128,1792]{1,0:T(8,128)(2,1)S(1)} collective-permute-done((bf16[128,1792]{1,0:T(8,128)(2,1)S(1)}, bf16[128,1792]{1,0:T(8,128)(2,1)S(1)}, u32[]{:S(2)}, u32[]{:S(2)}) %collective-permute-start.9) | collective-permute-done | bytes 458784 | tf_op jit(solution)/shard_map/ppermute | solution.py:29
  99.8 2.7 %collective-permute-start.12 = (bf16[128,1792]{1,0:T(8,128)(2,1)}, bf16[128,1792]{1,0:T(8,128)(2,1)}, u32[]{:S(2)}, u32[]{:S(2)}) collective-permute-start(bf16[128,1792]{1,0:T(8,128)(2,1)} %slice.85), channel_id=1, source_target_pairs={{0,129},{128,0},{1,128},{129,1},{2,131},{130,2},{3,130},{131,3},{4... | collective-permute-start | bytes 1376264 | tf_op jit(solution)/shard_map/ppermute | solution.py:29
  102.6 2.7 %collective-permute-start.18 = (bf16[256,1792]{1,0:T(8,128)(2,1)}, bf16[256,1792]{1,0:T(8,128)(2,1)}, u32[]{:S(2)}, u32[]{:S(2)}) collective-permute-start(bf16[256,1792]{1,0:T(8,128)(2,1)} %bitcast.17.own), channel_id=1, source_target_pairs={{0,129},{128,0},{1,128},{129,1},{2,131},{130,2},{3,130},{131,3},{4... | collective-permute-start | bytes 2752520 | tf_op jit(solution)/shard_map/ppermute | solution.py:29
  113.3 2.9 %near_sums.2.sums = f32[256,512]{1,0:T(8,128)S(1)} custom-call(bf16[256,1792]{1,0:T(8,128)(2,1)} %bitcast.5.own, bf16[256,1792]{1,0:T(8,128)(2,1)S(1)} %copy-done.20, bf16[256,1792]{1,0:T(8,128)(2,1)S(1)} %copy-done.22, bf16[1792,256]{1,0:T(8,128)(2,1)S(1)} %copy-done.3, bf16[1792,256]{1,0:T(8,128)(2,1)S(1)} %copy-done.1, bf16[1792,256]{1,0:T(8,128)(2,1)S(1)} %copy-done.5, ...), custom_call_target="tpu_custom_call" | custom-call | flops 1409286144 | bytes 5505024 | tf_op jit(solution)/shard_map/near_sums/pallas_call | solution.py:89
  118.4 2.7 %collective-permute-start.14 = (bf16[256,256]{1,0:T(8,128)(2,1)S(1)}, bf16[256,256]{1,0:T(8,128)(2,1)S(1)}, u32[]{:S(2)}, u32[]{:S(2)}) collective-permute-start(bf16[256,256]{1,0:T(8,128)(2,1)S(1)} %hidden_units.2.refs_0_), channel_id=1, source_target_pairs={{0,129},{128,0},{1,128},{129,1},{2,131},{130,2},{3,130},{131,3},{4... | collective-permute-start | bytes 393224 | tf_op jit(solution)/shard_map/ppermute | solution.py:29
  121.5 12.5 %collective-permute-done.13.refs_1_ = bf16[256,256]{1,0:T(8,128)(2,1)S(1)} collective-permute-done((bf16[256,256]{1,0:T(8,128)(2,1)S(1)}, bf16[256,256]{1,0:T(8,128)(2,1)S(1)}, u32[]{:S(2)}, u32[]{:S(2)}) %collective-permute-start.13) | collective-permute-done | bytes 131104 | tf_op jit(solution)/shard_map/ppermute | solution.py:29
  137.3 3.7 %down_product.2 = bf16[256,2432]{1,0:T(8,128)(2,1)S(1)} custom-call(bf16[256,256]{1,0:T(8,128)(2,1)S(1)} %hidden_units.2.refs_0_, bf16[256,256]{1,0:T(8,128)(2,1)S(1)} %collective-permute-done.13.refs_1_, bf16[256,256]{1,0:T(8,128)(2,1)S(1)} %collective-permute-done.14.refs_2_, bf16[256,256]{1,0:T(8,128)(2,1)S(1)} %collective-permute-done.15.refs_3_, ...), custom_call_target="tpu_custom_call" | custom-call | flops 939524096 | bytes 3670016 | tf_op jit(solution)/shard_map/down_product/pallas_call | solution.py:156
  142.1 8.8 %all-to-all-start.3 = ((bf16[32,8,2432]{2,1,0:T(8,128)(2,1)}), bf16[32,8,2432]{2,1,0:T(8,128)(2,1)}, u32[]{:S(2)}, u32[]{:S(2)}) async-start(bf16[32,8,2432]{2,1,0:T(8,128)(2,1)} %bitcast.66), calls=%async_computation.3 | async-start | bytes 2490368 | tf_op jit(solution)/shard_map/all_to_all | solution.py:39
  159.0 3.5 %near_sums.3.sums = f32[256,512]{1,0:T(8,128)S(1)} custom-call(bf16[256,1792]{1,0:T(8,128)(2,1)} %bitcast.17.own, bf16[256,1792]{1,0:T(8,128)(2,1)} %collective-permute-done.17.below, bf16[256,1792]{1,0:T(8,128)(2,1)} %collective-permute-done.18.above, bf16[1792,256]{1,0:T(8,128)(2,1)S(1)} %copy-done.4, bf16[1792,256]{1,0:T(8,128)(2,1)S(1)} %copy-done.2, ...), custom_call_target="tpu_custom_call" | custom-call | flops 1409286144 | bytes 5505024 | tf_op jit(solution)/shard_map/near_sums/pallas_call | solution.py:89
  172.2 2.6 %collective-permute-done.23.refs_3_ = bf16[256,256]{1,0:T(8,128)(2,1)S(1)} collective-permute-done((bf16[256,256]{1,0:T(8,128)(2,1)S(1)}, bf16[256,256]{1,0:T(8,128)(2,1)S(1)}, u32[]{:S(2)}, u32[]{:S(2)}) %collective-permute-start.23) | collective-permute-done | bytes 131104 | tf_op jit(solution)/shard_map/ppermute | solution.py:29
  174.9 4.6 %down_product.3 = bf16[256,1792]{1,0:T(8,128)(2,1)} custom-call(bf16[256,256]{1,0:T(8,128)(2,1)S(1)} %hidden_units.3.refs_0_, bf16[256,256]{1,0:T(8,128)(2,1)S(1)} %collective-permute-done.21.refs_1_, bf16[256,256]{1,0:T(8,128)(2,1)S(1)} %collective-permute-done.22.refs_2_, bf16[256,256]{1,0:T(8,128)(2,1)S(1)} %collective-permute-done.23.refs_3_, ...), custom_call_target="tpu_custom_call" | custom-call | flops 939524096 | bytes 3670016 | tf_op jit(solution)/shard_map/down_product/pallas_call | solution.py:156
  179.5 9.4 %all-to-all-start.2 = ((bf16[32,8,1792]{2,1,0:T(8,128)(2,1)}), bf16[32,8,1792]{2,1,0:T(8,128)(2,1)S(1)}, u32[]{:S(2)}, u32[]{:S(2)}) async-start(bf16[32,8,1792]{2,1,0:T(8,128)(2,1)} %bitcast.18), calls=%async_computation.2 | async-start | bytes 1835008 | tf_op jit(solution)/shard_map/all_to_all | solution.py:39
  198.5 8.0 %all-to-all-done.2 = bf16[32,8,1792]{2,1,0:T(8,128)(2,1)S(1)} async-done(((bf16[32,8,1792]{2,1,0:T(8,128)(2,1)}), bf16[32,8,1792]{2,1,0:T(8,128)(2,1)S(1)}, u32[]{:S(2)}, u32[]{:S(2)}) %all-to-all-start.2) | async-done | bytes 917536 | tf_op jit(solution)/shard_map/all_to_all | solution.py:39
  207.1 9.1 %collective-permute-start.24 = (bf16[32,1792]{1,0:T(8,128)(2,1)S(1)}, bf16[32,1792]{1,0:T(8,128)(2,1)S(1)}, u32[]{:S(2)}, u32[]{:S(2)}) collective-permute-start(bf16[32,1792]{1,0:T(8,128)(2,1)S(1)} %slice.139), channel_id=1, source_target_pairs={{0,2},{2,0},{4,6},{6,4},{8,10},{10,8},{12,14},{14,12},{16,18},{18,... | collective-permute-start | bytes 344072 | tf_op jit(solution)/shard_map/ppermute | solution.py:33
  (222 shorter events, 70.2 us)
Async XLA Ops:
  1.9 8.0 %collective-permute-start.3 = (f32[32]{0:T(128)S(1)}, f32[32]{0:T(128)S(1)}, u32[]{:S(2)}, u32[]{:S(2)}) collective-permute-start(f32[32]{0:T(128)S(1)} %reduce_sum.57), channel_id=1, source_target_pairs={{0,129},{128,0},{1,128},{129,1},{2,131},{130,2},{3,130},{131,3},{4... | collective-permute-start | bytes 392 | tf_op jit(solution)/shard_map/ppermute | solution.py:29
  7.3 5.4 %collective-permute-start = (f32[32,16]{1,0:T(8,128)S(1)}, f32[32,16]{1,0:T(8,128)S(1)}, u32[]{:S(2)}, u32[]{:S(2)}) collective-permute-start(f32[32,16]{1,0:T(8,128)S(1)} %add_convert_fusion), channel_id=1, source_target_pairs={{0,2},{2,0},{4,6},{6,4},{8,10},{10,8},{12,14},{14,12},{16,18},{18,... | collective-permute-start | bytes 6152 | tf_op jit(solution)/shard_map/ppermute | solution.py:33
  16.6 35.8 %all-to-all-start = ((bf16[32,8,1792]{2,1,0:T(8,128)(2,1)}), bf16[32,8,1792]{2,1,0:T(8,128)(2,1)}, u32[]{:S(2)}, u32[]{:S(2)}) async-start(bf16[32,8,1792]{2,1,0:T(8,128)(2,1)} %fusion), calls=%async_computation | async-start | bytes 1835008 | tf_op jit(solution)/shard_map/all_to_all | solution.py:39
  33.3 32.9 %collective-permute-start.7 = (bf16[384,1792]{1,0:T(8,128)(2,1)}, bf16[384,1792]{1,0:T(8,128)(2,1)S(1)}, u32[]{:S(2)}, u32[]{:S(2)}) collective-permute-start(bf16[384,1792]{1,0:T(8,128)(2,1)} %pad_maximum_fusion), channel_id=1, source_target_pairs={{0,128},{128,1},{1,129},{129,0},{2,130},{130,3},{3,131},{131,2},{4... | collective-permute-start | bytes 4128776 | tf_op jit(solution)/shard_map/ppermute | solution.py:29
  34.5 31.9 %collective-permute-start.8 = (bf16[384,1792]{1,0:T(8,128)(2,1)}, bf16[384,1792]{1,0:T(8,128)(2,1)}, u32[]{:S(2)}, u32[]{:S(2)}) collective-permute-start(bf16[384,1792]{1,0:T(8,128)(2,1)} %pad_maximum_fusion.1), channel_id=1, source_target_pairs={{0,129},{128,0},{1,128},{129,1},{2,131},{130,2},{3,130},{131,3},{4... | collective-permute-start | bytes 4128776 | tf_op jit(solution)/shard_map/ppermute | solution.py:29
  52.4 50.2 %all-to-all-start.1 = ((bf16[32,8,1792]{2,1,0:T(8,128)(2,1)}), bf16[32,8,1792]{2,1,0:T(8,128)(2,1)}, u32[]{:S(2)}, u32[]{:S(2)}) async-start(bf16[32,8,1792]{2,1,0:T(8,128)(2,1)} %bitcast.69), calls=%async_computation.1 | async-start | bytes 1835008 | tf_op jit(solution)/shard_map/all_to_all | solution.py:39
  57.9 5.4 %collective-permute-start.16 = (bf16[128,640]{0,1:T(8,128)(2,1)S(1)}, bf16[128,640]{0,1:T(8,128)(2,1)S(1)}, u32[]{:S(2)}, u32[]{:S(2)}) collective-permute-start(bf16[128,640]{0,1:T(8,128)(2,1)S(1)} %pad_maximum_fusion.3), channel_id=1, source_target_pairs={{0,2},{2,0},{4,6},{6,4},{8,10},{10,8},{12,14},{14,12},{16,18},{18,... | collective-permute-start | bytes 491528 | tf_op jit(solution)/shard_map/ppermute | solution.py:33
  60.6 36.7 %collective-permute-start.5 = (bf16[256,1792]{1,0:T(8,128)(2,1)}, bf16[256,1792]{1,0:T(8,128)(2,1)S(1)}, u32[]{:S(2)}, u32[]{:S(2)}) collective-permute-start(bf16[256,1792]{1,0:T(8,128)(2,1)} %bitcast.5.own), channel_id=1, source_target_pairs={{0,128},{128,1},{1,129},{129,0},{2,130},{130,3},{3,131},{131,2},{4... | collective-permute-start | bytes 2752520 | tf_op jit(solution)/shard_map/ppermute | solution.py:29
  60.6 36.7 %collective-permute-start.6 = (bf16[256,1792]{1,0:T(8,128)(2,1)}, bf16[256,1792]{1,0:T(8,128)(2,1)S(1)}, u32[]{:S(2)}, u32[]{:S(2)}) collective-permute-start(bf16[256,1792]{1,0:T(8,128)(2,1)} %bitcast.5.own), channel_id=1, source_target_pairs={{0,129},{128,0},{1,128},{129,1},{2,131},{130,2},{3,130},{131,3},{4... | collective-permute-start | bytes 2752520 | tf_op jit(solution)/shard_map/ppermute | solution.py:29
  66.2 29.5 %collective-permute-start.9 = (bf16[128,1792]{1,0:T(8,128)(2,1)S(1)}, bf16[128,1792]{1,0:T(8,128)(2,1)S(1)}, u32[]{:S(2)}, u32[]{:S(2)}) collective-permute-start(bf16[128,1792]{1,0:T(8,128)(2,1)S(1)} %slice.102), channel_id=1, source_target_pairs={{0,128},{128,1},{1,129},{129,0},{2,130},{130,3},{3,131},{131,2},{4... | collective-permute-start | bytes 1376264 | tf_op jit(solution)/shard_map/ppermute | solution.py:29
  67.7 28.7 %collective-permute-start.10 = (bf16[128,1792]{1,0:T(8,128)(2,1)S(1)}, bf16[128,1792]{1,0:T(8,128)(2,1)S(1)}, u32[]{:S(2)}, u32[]{:S(2)}) collective-permute-start(bf16[128,1792]{1,0:T(8,128)(2,1)S(1)} %slice.103), channel_id=1, source_target_pairs={{0,129},{128,0},{1,128},{129,1},{2,131},{130,2},{3,130},{131,3},{4... | collective-permute-start | bytes 1376264 | tf_op jit(solution)/shard_map/ppermute | solution.py:29
  99.0 17.3 %collective-permute-start.11 = (bf16[128,1792]{1,0:T(8,128)(2,1)}, bf16[128,1792]{1,0:T(8,128)(2,1)}, u32[]{:S(2)}, u32[]{:S(2)}) collective-permute-start(bf16[128,1792]{1,0:T(8,128)(2,1)} %slice.84), channel_id=1, source_target_pairs={{0,128},{128,1},{1,129},{129,0},{2,130},{130,3},{3,131},{131,2},{4... | collective-permute-start | bytes 1376264 | tf_op jit(solution)/shard_map/ppermute | solution.py:29
  99.8 16.5 %collective-permute-start.12 = (bf16[128,1792]{1,0:T(8,128)(2,1)}, bf16[128,1792]{1,0:T(8,128)(2,1)}, u32[]{:S(2)}, u32[]{:S(2)}) collective-permute-start(bf16[128,1792]{1,0:T(8,128)(2,1)} %slice.85), channel_id=1, source_target_pairs={{0,129},{128,0},{1,128},{129,1},{2,131},{130,2},{3,130},{131,3},{4... | collective-permute-start | bytes 1376264 | tf_op jit(solution)/shard_map/ppermute | solution.py:29
  102.6 39.5 %collective-permute-start.17 = (bf16[256,1792]{1,0:T(8,128)(2,1)}, bf16[256,1792]{1,0:T(8,128)(2,1)}, u32[]{:S(2)}, u32[]{:S(2)}) collective-permute-start(bf16[256,1792]{1,0:T(8,128)(2,1)} %bitcast.17.own), channel_id=1, source_target_pairs={{0,128},{128,1},{1,129},{129,0},{2,130},{130,3},{3,131},{131,2},{4... | collective-permute-start | bytes 2752520 | tf_op jit(solution)/shard_map/ppermute | solution.py:29
  102.6 39.5 %collective-permute-start.18 = (bf16[256,1792]{1,0:T(8,128)(2,1)}, bf16[256,1792]{1,0:T(8,128)(2,1)}, u32[]{:S(2)}, u32[]{:S(2)}) collective-permute-start(bf16[256,1792]{1,0:T(8,128)(2,1)} %bitcast.17.own), channel_id=1, source_target_pairs={{0,129},{128,0},{1,128},{129,1},{2,131},{130,2},{3,130},{131,3},{4... | collective-permute-start | bytes 2752520 | tf_op jit(solution)/shard_map/ppermute | solution.py:29
  118.3 15.6 %collective-permute-start.13 = (bf16[256,256]{1,0:T(8,128)(2,1)S(1)}, bf16[256,256]{1,0:T(8,128)(2,1)S(1)}, u32[]{:S(2)}, u32[]{:S(2)}) collective-permute-start(bf16[256,256]{1,0:T(8,128)(2,1)S(1)} %hidden_units.2.refs_0_), channel_id=1, source_target_pairs={{0,128},{128,1},{1,129},{129,0},{2,130},{130,3},{3,131},{131,2},{4... | collective-permute-start | bytes 393224 | tf_op jit(solution)/shard_map/ppermute | solution.py:29
  118.4 16.5 %collective-permute-start.14 = (bf16[256,256]{1,0:T(8,128)(2,1)S(1)}, bf16[256,256]{1,0:T(8,128)(2,1)S(1)}, u32[]{:S(2)}, u32[]{:S(2)}) collective-permute-start(bf16[256,256]{1,0:T(8,128)(2,1)S(1)} %hidden_units.2.refs_0_), channel_id=1, source_target_pairs={{0,129},{128,0},{1,128},{129,1},{2,131},{130,2},{3,130},{131,3},{4... | collective-permute-start | bytes 393224 | tf_op jit(solution)/shard_map/ppermute | solution.py:29
  121.1 16.2 %collective-permute-start.15 = (bf16[256,256]{1,0:T(8,128)(2,1)S(1)}, bf16[256,256]{1,0:T(8,128)(2,1)S(1)}, u32[]{:S(2)}, u32[]{:S(2)}) collective-permute-start(bf16[256,256]{1,0:T(8,128)(2,1)S(1)} %hidden_units.2.refs_0_), channel_id=1, source_target_pairs={{0,1},{128,129},{1,0},{129,128},{2,3},{130,131},{3,2},{131,130},{4... | collective-permute-start | bytes 393224 | tf_op jit(solution)/shard_map/ppermute | solution.py:29
  142.1 37.4 %all-to-all-start.3 = ((bf16[32,8,2432]{2,1,0:T(8,128)(2,1)}), bf16[32,8,2432]{2,1,0:T(8,128)(2,1)}, u32[]{:S(2)}, u32[]{:S(2)}) async-start(bf16[32,8,2432]{2,1,0:T(8,128)(2,1)} %bitcast.66), calls=%async_computation.3 | async-start | bytes 2490368 | tf_op jit(solution)/shard_map/all_to_all | solution.py:39
  154.9 10.2 %collective-permute-start.19 = (bf16[128,1792]{1,0:T(8,128)(2,1)S(1)}, bf16[128,1792]{1,0:T(8,128)(2,1)S(1)}, u32[]{:S(2)}, u32[]{:S(2)}) collective-permute-start(bf16[128,1792]{1,0:T(8,128)(2,1)S(1)} %slice.87), channel_id=1, source_target_pairs={{0,128},{128,1},{1,129},{129,0},{2,130},{130,3},{3,131},{131,2},{4... | collective-permute-start | bytes 1376264 | tf_op jit(solution)/shard_map/ppermute | solution.py:29
  157.4 8.4 %collective-permute-start.20 = (bf16[128,1792]{1,0:T(8,128)(2,1)S(1)}, bf16[128,1792]{1,0:T(8,128)(2,1)S(1)}, u32[]{:S(2)}, u32[]{:S(2)}) collective-permute-start(bf16[128,1792]{1,0:T(8,128)(2,1)S(1)} %slice.88), channel_id=1, source_target_pairs={{0,129},{128,0},{1,128},{129,1},{2,131},{130,2},{3,130},{131,3},{4... | collective-permute-start | bytes 1376264 | tf_op jit(solution)/shard_map/ppermute | solution.py:29
  166.5 5.7 %collective-permute-start.21 = (bf16[256,256]{1,0:T(8,128)(2,1)S(1)}, bf16[256,256]{1,0:T(8,128)(2,1)S(1)}, u32[]{:S(2)}, u32[]{:S(2)}) collective-permute-start(bf16[256,256]{1,0:T(8,128)(2,1)S(1)} %hidden_units.3.refs_0_), channel_id=1, source_target_pairs={{0,128},{128,1},{1,129},{129,0},{2,130},{130,3},{3,131},{131,2},{4... | collective-permute-start | bytes 393224 | tf_op jit(solution)/shard_map/ppermute | solution.py:29
  179.5 27.0 %all-to-all-start.2 = ((bf16[32,8,1792]{2,1,0:T(8,128)(2,1)}), bf16[32,8,1792]{2,1,0:T(8,128)(2,1)S(1)}, u32[]{:S(2)}, u32[]{:S(2)}) async-start(bf16[32,8,1792]{2,1,0:T(8,128)(2,1)} %bitcast.18), calls=%async_computation.2 | async-start | bytes 1835008 | tf_op jit(solution)/shard_map/all_to_all | solution.py:39
  207.1 10.1 %collective-permute-start.24 = (bf16[32,1792]{1,0:T(8,128)(2,1)S(1)}, bf16[32,1792]{1,0:T(8,128)(2,1)S(1)}, u32[]{:S(2)}, u32[]{:S(2)}) collective-permute-start(bf16[32,1792]{1,0:T(8,128)(2,1)S(1)} %slice.139), channel_id=1, source_target_pairs={{0,2},{2,0},{4,6},{6,4},{8,10},{10,8},{12,14},{14,12},{16,18},{18,... | collective-permute-start | bytes 344072 | tf_op jit(solution)/shard_map/ppermute | solution.py:33
  (60 other events, 641.6 us)
where the time goes:
time: 219 us; the launch traced here: 218 us
  starting transfers between devices  77.7 us (35%)
  waiting for transfers between devices  68.1 us (31%)
  local copies, waits for them, and re-layouts  30.5 us (14%)
  Pallas kernels  17.4 us (8%)
  matrix products  14.2 us (6%)
  other arithmetic  8.34 us (4%)
    ppermute x21, waiting for transfers between devices, over_y(): return lax.ppermute(v, GROUP, y_perm(k % NY)) if k % NY else v  45.2 us
    all_to_all x4, starting transfers between devices, chips_exchange(): lax.all_to_all(v, 'ep', split_axis=0, concat_axis=0, tiled=True, axis_ind...  34.7 us
    ppermute x21, starting transfers between devices, over_y(): return lax.ppermute(v, GROUP, y_perm(k % NY)) if k % NY else v  28.4 us
    all_to_all x4, waiting for transfers between devices, chips_exchange(): lax.all_to_all(v, 'ep', split_axis=0, concat_axis=0, tiled=True, axis_ind...  21.9 us
    ppermute x4, starting transfers between devices, other_core(): lax.ppermute(v, 'ep', [(i, i ^ 1) for i in range(lax.axis_size('ep'))])  14.6 us
    unnamed x110, local copies, waits for them, and re-layouts  12.3 us
    pallas_call x2, Pallas kernels, down_product(): pl.pallas_call(lambda *refs: down_kernel(len(hidden), len(downs), *refs),...  8.4 us
    pallas_call x2, Pallas kernels, near_sums(): pl.pallas_call(near_kernel, out_shape=jax.ShapeDtypeStruct((n, 2 * cols),...  6.34 us
  transfers between devices with their start and end apart: 29, of which 13 were waited for; matrix products, arithmetic and copies ran while one was open for 17% of the time, Pallas kernels for 8%

commit v1 on v0

--- a/solution.py
+++ b/solution.py
@@ -99,23 +99,24 @@
     )(own, below, above, *weights)
 
 
-def hidden_kernel(low, high, sums, gate_w, up_w, out):
+def hidden_kernel(low, high, sums, factor, gate_w, up_w, out):
     n, cols = out.shape
     mid = n // 2
     for rows, first in ((low, 0), (high, mid)):
         at = slice(first, first + mid)
         gate = sums[at, :cols] + dot(rows[...], gate_w[...])
         up = sums[at, cols:] + dot(rows[...], up_w[...])
+        gate, up = gate * factor[at, :], up * factor[at, :]
         out[at, :] = (gate / (1.0 + jnp.exp(-gate)) * up).astype(out.dtype)
 
 
-def hidden_units(low, high, sums, gate_w, up_w):
+def hidden_units(low, high, sums, factor, gate_w, up_w):
     mid, depth = low.shape
     cols = gate_w.shape[1]
     return pl.pallas_call(
         hidden_kernel,
         out_shape=jax.ShapeDtypeStruct((2 * mid, cols), jnp.bfloat16),
-        in_specs=[WHOLE] * 5,
+        in_specs=[WHOLE] * 6,
         out_specs=WHOLE,
         compiler_params=pltpu.CompilerParams(vmem_limit_bytes=SCOPED),
         cost_estimate=pl.CostEstimate(
@@ -124,41 +125,31 @@
             transcendentals=2 * mid * cols,
         ),
         name="hidden_units",
-    )(low, high, sums, gate_w, up_w)
+    )(low, high, sums, factor, gate_w, up_w)
 
 
 def down_kernel(n_hidden, n_downs, *refs):
     hidden, downs = refs[:n_hidden], refs[n_hidden : n_hidden + n_downs]
     out = refs[-1]
-    depth, cols = downs[0].shape
+    cols = downs[0].shape[1]
     tile = 256 if cols % 256 == 0 else 128
 
     @pl.loop(0, cols // tile)
     def _(step):
         at = pl.ds(pl.multiple_of(step * tile, tile), tile)
         total = 0.0
-        for k, w in enumerate(downs[:-2]):
-            total = total + dot(hidden[k][...], w[:depth, at])
-        rows = 0
-        for w in downs[-2:]:
-            total = total + dot(hidden[-1][:, rows : rows + w.shape[0]], w[:, at])
-            rows += w.shape[0]
+        for h, w in zip(hidden, downs):
+            total = total + dot(h[...], w[:, at])
         out[:, at] = total.astype(out.dtype)
 
-    if len(refs) > n_hidden + n_downs + 1:
-        out[:, cols:] = refs[-2][...]
-
-
-def down_product(hidden, downs, rider=None):
+
+def down_product(hidden, downs):
     n, depth = hidden[0].shape
     cols = downs[0].shape[1]
-    more = [] if rider is None else [rider]
     return pl.pallas_call(
         lambda *refs: down_kernel(len(hidden), len(downs), *refs),
-        out_shape=jax.ShapeDtypeStruct(
-            (n, cols + sum(v.shape[1] for v in more)), jnp.bfloat16
-        ),
-        in_specs=[WHOLE] * (len(hidden) + len(downs) + len(more)),
+        out_shape=jax.ShapeDtypeStruct((n, cols), jnp.bfloat16),
+        in_specs=[WHOLE] * (len(hidden) + len(downs)),
         out_specs=WHOLE,
         compiler_params=pltpu.CompilerParams(vmem_limit_bytes=SCOPED),
         cost_estimate=pl.CostEstimate(
@@ -167,7 +158,7 @@
             transcendentals=0,
         ),
         name="down_product",
-    )(*hidden, *downs, *more)
+    )(*hidden, *downs)
 
 
 def attention(got, old_cache, cache_len, new_latent, dec_query):
@@ -239,25 +230,21 @@
         return group_of_y((y + k) % NY)
 
     wide = dec_states.reshape(tok, d_part).astype(jnp.float32)
-    squares = jnp.sum(wide * wide, axis=1)
-    square_sum = squares
-    for k in range(1, NY):
-        square_sum = square_sum + over_y(squares, k)
-    scale = lax.rsqrt(square_sum / (d_part * NY) + EPS)[:, None]
-    normed = (wide * scale * moe_gain).astype(jnp.bfloat16)
-    kept, upward, downward, across = [
-        lax.dynamic_slice_in_dim(w_down[0], part_of(k) * d_part, d_part, axis=1) for k in ORDER
+    scaled = (wide * moe_gain).astype(jnp.bfloat16)
+    meta = jnp.concatenate(
+        [
+            expert_ids.reshape(tok, topk).astype(jnp.float32),
+            route_weight.reshape(tok, topk).astype(jnp.float32),
+            jnp.sum(wide * wide, axis=1, keepdims=True),
+        ],
+        axis=1,
+    )
+    meta = jnp.concatenate([meta, other_core(meta)], axis=0)
+    scaled = jnp.concatenate([scaled, other_core(scaled)], axis=0)
+    downs = [
+        over_y(lax.dynamic_slice_in_dim(w_down[0], part_of(k) * d_part, d_part, axis=1), k)
+        for k in ORDER
     ]
-    units = across.shape[0]
-    upward = jnp.concatenate([upward, across[: units // 2]], axis=0)
-    downward = jnp.concatenate([downward, across[units // 2 :]], axis=0)
-    upward, downward = over_y(upward, 1), over_y(downward, -1)
-    downs = [kept, upward, downward, over_y(upward[units:], 1), over_y(downward[units:], -1)]
-    meta = jnp.concatenate(
-        [expert_ids.reshape(tok, topk), route_weight.reshape(tok, topk)], axis=1
-    ).astype(jnp.float32)
-    meta = jnp.concatenate([meta, other_core(meta)], axis=0)
-    normed = jnp.concatenate([normed, other_core(normed)], axis=0)
     ids = meta[:, :topk].astype(jnp.int32)
     here = 2 * jnp.arange(chips, dtype=jnp.int32) + core
     named = ids.T[:, None, :] == here[None, :, None]
@@ -265,27 +252,55 @@
     half = E_CAP // CHUNKS
     n = chips * 2 * half
     chosen = [chosen[:, :, c * half : (c + 1) * half] for c in range(CHUNKS)]
-    picks = [v.astype(jnp.bfloat16).reshape(n, 2 * tok) for v in chosen]
+    pick = jnp.stack(chosen, axis=1).astype(jnp.bfloat16).reshape(CHUNKS * n, 2 * tok)
 
     def exchange(v):
-        return chips_exchange(v.reshape(chips, 2 * half, -1)).reshape(n, -1)
-
-    sends = [dot(pick, normed).astype(jnp.bfloat16) for pick in picks]
-    first = exchange(sends[0])
-    first, second, gate_w, up_w = lax.optimization_barrier(
-        (first, sends[1], w_gate[0], w_up[0])
-    )
+        return chips_exchange(v.reshape(chips, v.shape[0] // chips, -1))
+
+    rows = exchange(dot(pick, scaled).astype(jnp.bfloat16))
+    squares = meta[:, 2 * topk]
+    square_sum = squares
+    for k in range(1, NY):
+        square_sum = square_sum + over_y(squares, k)
+    scale = lax.rsqrt(square_sum / (d_part * NY) + EPS)
+    pieces, rest = [], scale
+    for _ in range(3):
+        pieces.append(lax.reduce_precision(rest, 8, 7))
+        rest = rest - pieces[-1]
+    pieces = jnp.stack(pieces, axis=1).astype(jnp.bfloat16)
+    scales = jnp.concatenate(
+        [dot(v.astype(jnp.bfloat16).reshape(n, 2 * tok), pieces) for v in chosen], axis=1
+    ).astype(jnp.bfloat16)
+    follow = jnp.concatenate([prompts[:, : -scales.shape[1]], scales], axis=1)
+    rows, downs, follow, gate_w, up_w = lax.optimization_barrier(
+        (rows, downs, follow, w_gate[0], w_up[0])
+    )
+    got = exchange(follow).reshape(n, -1)
+    attn_out = attend(got)
+    factors = [
+        jnp.sum(got[:, at : at + 3].astype(jnp.float32), axis=1, keepdims=True)
+        for at in (got.shape[1] - 6, got.shape[1] - 3)
+    ]
     blocks = [
         lax.dynamic_slice_in_dim(source, part_of(k) * d_part, d_part, axis=0)
         for k in (0, NY - 1, 1, 2)
         for source in (gate_w, up_w)
     ]
-    arrived = [first, exchange(second)]
+    arrived = [
+        rows[:, c * 2 * half : (c + 1) * 2 * half].reshape(n, d_part) for c in range(CHUNKS)
+    ]
 
     def neighbours(rows):
         return over_y(rows, 1), over_y(rows, -1)
 
-    near = [neighbours(rows) for rows in arrived]
+    def across(below, above):
+        mid = n // 2
+        return over_y(below[:mid], 1), over_y(above[mid:], -1)
+
+    near = [neighbours(arrived[0])]
+    near[0], arrived[1], blocks = lax.optimization_barrier((near[0], arrived[1], blocks))
+    near.append(neighbours(arrived[1]))
+    far = [across(*v) for v in near]
 
     weight = meta[:, topk : 2 * topk]
     share = weight / jnp.sum(weight, axis=1, keepdims=True)
@@ -299,24 +314,19 @@
     contract = (((0,), (0,)), ((), ()))
     for c in range(CHUNKS):
         below, above = near[c]
+        low, high = far[c]
+        sums = near_sums(arrived[c], below, above, blocks[:6])
+        hidden = hidden_units(low, high, sums, factors[c], *blocks[6:])
+        hidden = [over_y(hidden, k) for k in ORDER]
+        out = down_product(hidden, downs)
         if c == 0:
-            below, above, downs, blocks = lax.optimization_barrier((below, above, downs, blocks))
-        mid = n // 2
-        low, high = over_y(below[:mid], 1), over_y(above[mid:], -1)
-        sums = near_sums(arrived[c], below, above, blocks[:6])
-        hidden = hidden_units(low, high, sums, *blocks[6:])
-        hidden = [over_y(hidden, k) for k in ORDER]
-        out = down_product(hidden, downs, prompts if c == 0 else None)
-        if c == 0:
-            out, *near[1] = lax.optimization_barrier((out, *near[1]))
-        back = exchange(out)
-        if c == 0:
-            attn_out = attend(back[:, d_part:])
-        else:
+            out, near[1], far[1] = lax.optimization_barrier((out, near[1], far[1]))
+        back = exchange(out).reshape(n, -1)
+        if c == 1:
             back, attn_out, mixed, mixes = lax.optimization_barrier((back, attn_out, mixed, mixes))
         for part in mixes[c]:
             mixed = mixed + lax.dot_general(
-                part, back[:, :d_part], contract, preferred_element_type=jnp.float32
+                part, back, contract, preferred_element_type=jnp.float32
             )
     mixed = mixed[:tok] + other_core(mixed[tok:].astype(jnp.bfloat16)).astype(jnp.float32)
     return mixed.astype(jnp.bfloat16).reshape(seq_dev, steps, d_part), attn_out

time: 219 us -> 215 us (0.982)
  waiting for transfers between devices: 68.1 us -> 56.9 us
  matrix products: 14.2 us -> 17.2 us
  local copies, waits for them, and re-layouts: 30.5 us -> 33.3 us
  other arithmetic: 8.34 us -> 10.9 us
    all_to_all x4, waiting for transfers between devices: 21.9 us -> 9.71 us  [chips_exchange(): lax.all_to_all(v, 'ep', split_axis=0, concat_axis=0, tiled=True, axis_ind...]
    unnamed x110 -> x116, local copies, waits for them, and re-layouts: 12.3 us -> 9.04 us
    ppermute x21 -> x20, starting transfers between devices: 28.4 us -> 25.3 us  [over_y(): return lax.ppermute(v, GROUP, y_perm(k % NY)) if k % NY else v]
    reshape x0 -> x1, local copies, waits for them, and re-layouts: none -> 2.81 us  [experts(): rows[:, c * 2 * half:(c + 1) * 2 * half].reshape(n, d_part)]
    dot_general x5 -> x6, matrix products: 3.35 us -> 5.39 us  [dot(): return jnp.dot(a, b, preferred_element_type=jnp.float32)]
    ppermute x21 -> x20, waiting for transfers between devices: 45.2 us -> 46.2 us  [over_y(): return lax.ppermute(v, GROUP, y_perm(k % NY)) if k % NY else v]
    slice x7 -> x4, local copies, waits for them, and re-layouts: 6.45 us -> 5.87 us  [across(): return (over_y(below[:mid], 1), over_y(above[mid:], -1))]
  transfers between devices with their start and end apart: 29 -> 28, of which waited for: 13 -> 11; matrix products, arithmetic and copies ran while one was open for 17% -> 20% of each run, Pallas kernels for 8% -> 8%
where the time goes in v1:
time: 215 us; the launch traced here: 213 us
  starting transfers between devices  76.2 us (35%)
  waiting for transfers between devices  56.9 us (26%)
  local copies, waits for them, and re-layouts  33.3 us (15%)
  matrix products  17.2 us (8%)
  Pallas kernels  16.9 us (8%)
  other arithmetic  10.9 us (5%)
    ppermute x20, waiting for transfers between devices, over_y(): return lax.ppermute(v, GROUP, y_perm(k % NY)) if k % NY else v  46.2 us
    all_to_all x4, starting transfers between devices, chips_exchange(): lax.all_to_all(v, 'ep', split_axis=0, concat_axis=0, tiled=True, axis_ind...  35.4 us
    ppermute x20, starting transfers between devices, over_y(): return lax.ppermute(v, GROUP, y_perm(k % NY)) if k % NY else v  25.3 us
    ppermute x4, starting transfers between devices, other_core(): lax.ppermute(v, 'ep', [(i, i ^ 1) for i in range(lax.axis_size('ep'))])  15.5 us
    all_to_all x4, waiting for transfers between devices, chips_exchange(): lax.all_to_all(v, 'ep', split_axis=0, concat_axis=0, tiled=True, axis_ind...  9.71 us
    unnamed x116, local copies, waits for them, and re-layouts  9.04 us
    pallas_call x2, Pallas kernels, down_product(): pl.pallas_call(lambda *refs: down_kernel(len(hidden), len(downs), *refs),...  7.61 us
    pallas_call x2, Pallas kernels, near_sums(): pl.pallas_call(near_kernel, out_shape=jax.ShapeDtypeStruct((n, 2 * cols),...  6.78 us
  transfers between devices with their start and end apart: 28, of which 11 were waited for; matrix products, arithmetic and copies ran while one was open for 20% of the time, Pallas kernels for 8%

profile of v1, /device:TPU:1, one launch (start us, length us, event | category | flops | bytes accessed | tf_op | source)
XLA Modules:
  0.0 213.1 jit_solution(1369594401002117461)
XLA Ops:
  3.5 3.3 %collective-permute-start = (f32[32,17]{0,1:T(8,128)S(1)}, f32[32,17]{0,1:T(8,128)S(1)}, u32[]{:S(2)}, u32[]{:S(2)}) collective-permute-start(f32[32,17]{0,1:T(8,128)S(1)} %pad_maximum_fusion.2), channel_id=1, source_target_pairs={{0,2},{2,0},{4,6},{6,4},{8,10},{10,8},{12,14},{14,12},{16,18},{18,... | collective-permute-start | bytes 6536 | tf_op jit(solution)/shard_map/ppermute | solution.py:33
  12.4 9.4 %all-to-all-start = ((bf16[32,16,1792]{2,1,0:T(8,128)(2,1)}), bf16[32,16,1792]{2,1,0:T(8,128)(2,1)}, u32[]{:S(2)}, u32[]{:S(2)}) async-start(bf16[32,16,1792]{2,1,0:T(8,128)(2,1)} %bitcast.7), calls=%async_computation | async-start | bytes 3670016 | tf_op jit(solution)/shard_map/all_to_all | solution.py:39
  22.1 4.0 %dynamic-slice_bitcast_fusion = (bf16[256,1792]{1,0:T(8,128)(2,1)}, bf16[256,1792]{1,0:T(8,128)(2,1)}, bf16[256,1792]{1,0:T(8,128)(2,1)}, bf16[256,1792]{1,0:T(8,128)(2,1)}) fusion(bf16[1,256,7168]{2,1,0:T(8,128)(2,1)} %param.27, s32[]{:T(128)S(6)} %select_n.258, s32[]{:T(128)S(6)} %select_n.248, s32[]{:T(128)S(6)} %select_n.243, s32[]{:T(128)S(6)} %select_n.253), kind=kLoop, calls=%fused_computation.24 | loop fusion | bytes 7340048 | tf_op jit(solution)/shard_map/dynamic_slice | solution.py:245
  33.4 15.1 %collective-permute-done.8 = f32[64]{0:T(128)S(1)} collective-permute-done((f32[64]{0:T(128)}, f32[64]{0:T(128)S(1)}, u32[]{:S(2)}, u32[]{:S(2)}) %collective-permute-start.8) | collective-permute-done | bytes 288 | tf_op jit(solution)/shard_map/ppermute | solution.py:29
  48.5 2.6 %collective-permute-start.4 = (bf16[256,1792]{1,0:T(8,128)(2,1)}, bf16[256,1792]{1,0:T(8,128)(2,1)}, u32[]{:S(2)}, u32[]{:S(2)}) collective-permute-start(bf16[256,1792]{1,0:T(8,128)(2,1)} %get-tuple-element.74), channel_id=1, source_target_pairs={{0,1},{128,129},{1,0},{129,128},{2,3},{130,131},{3,2},{131,130},{4... | collective-permute-start | bytes 2752520 | tf_op jit(solution)/shard_map/ppermute | solution.py:29
  62.3 7.9 %collective-permute-done.4.refs_7_ = bf16[256,1792]{1,0:T(8,128)(2,1)} collective-permute-done((bf16[256,1792]{1,0:T(8,128)(2,1)}, bf16[256,1792]{1,0:T(8,128)(2,1)}, u32[]{:S(2)}, u32[]{:S(2)}) %collective-permute-start.4) | collective-permute-done | bytes 917536 | tf_op jit(solution)/shard_map/ppermute | solution.py:29
  70.3 2.8 %slice_bitcast_fusion = (bf16[256,1792]{1,0:T(8,128)(2,1)}, bf16[256,1792]{1,0:T(8,128)(2,1)}) fusion(bf16[32,16,1792]{2,1,0:T(8,128)(2,1)} %all-to-all-done), kind=kLoop, calls=%fused_computation.22 | loop fusion | bytes 3670016 | tf_op jit(solution)/shard_map/reshape | solution.py:290
  76.1 8.6 %all-to-all-start.1 = ((bf16[32,8,640]{2,1,0:T(8,128)(2,1)}), bf16[32,8,640]{2,1,0:T(8,128)(2,1)S(1)}, u32[]{:S(2)}, u32[]{:S(2)}) async-start(bf16[32,8,640]{2,1,0:T(8,128)(2,1)} %bitcast.99), calls=%async_computation.1 | async-start | bytes 655360 | tf_op jit(solution)/shard_map/all_to_all | solution.py:39
  84.6 5.8 %constant_dynamic-slice_fusion = (bf16[1792,256]{1,0:T(8,128)(2,1)}, bf16[1792,256]{1,0:T(8,128)(2,1)S(1)}, bf16[1792,256]{1,0:T(8,128)(2,1)S(1)}, bf16[1792,256...) fusion(bf16[7168,256]{1,0:T(8,128)(2,1)} %bitcast.93, ...), kind=kLoop, calls=%fused_computation.103 | loop fusion | bytes 14680080 | tf_op jit(solution)/shard_map/dynamic_slice | solution.py:285
  90.4 3.5 %collective-permute-done.9.below = bf16[256,1792]{1,0:T(8,128)(2,1)} collective-permute-done((bf16[256,1792]{1,0:T(8,128)(2,1)}, bf16[256,1792]{1,0:T(8,128)(2,1)}, u32[]{:S(2)}, u32[]{:S(2)}) %collective-permute-start.9) | collective-permute-done | bytes 917536 | tf_op jit(solution)/shard_map/ppermute | solution.py:29
  101.7 2.7 %collective-permute-start.12 = (bf16[128,1792]{1,0:T(8,128)(2,1)}, bf16[128,1792]{1,0:T(8,128)(2,1)}, u32[]{:S(2)}, u32[]{:S(2)}) collective-permute-start(bf16[128,1792]{1,0:T(8,128)(2,1)} %slice.77), channel_id=1, source_target_pairs={{0,129},{128,0},{1,128},{129,1},{2,131},{130,2},{3,130},{131,3},{4... | collective-permute-start | bytes 1376264 | tf_op jit(solution)/shard_map/ppermute | solution.py:29
  111.2 3.3 %near_sums.2.sums = f32[256,512]{1,0:T(8,128)S(1)} custom-call(bf16[256,1792]{1,0:T(8,128)(2,1)} %get-tuple-element.79.own, bf16[256,1792]{1,0:T(8,128)(2,1)} %collective-permute-done.9.below, bf16[256,1792]{1,0:T(8,128)(2,1)} %collective-permute-done.10.above, bf16[1792,256]{1,0:T(8,128)(2,1)S(1)} %copy-done.3, bf16[1792,256]{1,0:T(8,128)(2,1)S(1)} %copy-done.1, ...), custom_call_target="tpu_custom_call" | custom-call | flops 1409286144 | bytes 5505024 | tf_op jit(solution)/shard_map/near_sums/pallas_call | solution.py:89
  116.9 2.7 %collective-permute-start.19 = (bf16[128,1792]{1,0:T(8,128)(2,1)S(1)}, bf16[128,1792]{1,0:T(8,128)(2,1)S(1)}, u32[]{:S(2)}, u32[]{:S(2)}) collective-permute-start(bf16[128,1792]{1,0:T(8,128)(2,1)S(1)} %slice.96), channel_id=1, source_target_pairs={{0,129},{128,0},{1,128},{129,1},{2,131},{130,2},{3,130},{131,3},{4... | collective-permute-start | bytes 1376264 | tf_op jit(solution)/shard_map/ppermute | solution.py:29
  119.7 3.8 %collective-permute-done.11.low = bf16[128,1792]{1,0:T(8,128)(2,1)} collective-permute-done((bf16[128,1792]{1,0:T(8,128)(2,1)}, bf16[128,1792]{1,0:T(8,128)(2,1)}, u32[]{:S(2)}, u32[]{:S(2)}) %collective-permute-start.11) | collective-permute-done | bytes 458784 | tf_op jit(solution)/shard_map/ppermute | solution.py:29
  129.1 6.9 %collective-permute-done.13.refs_1_ = bf16[256,256]{1,0:T(8,128)(2,1)S(1)} collective-permute-done((bf16[256,256]{1,0:T(8,128)(2,1)S(1)}, bf16[256,256]{1,0:T(8,128)(2,1)S(1)}, u32[]{:S(2)}, u32[]{:S(2)}) %collective-permute-start.13) | collective-permute-done | bytes 131104 | tf_op jit(solution)/shard_map/ppermute | solution.py:29
  136.0 3.4 %collective-permute-done.15.refs_3_ = bf16[256,256]{1,0:T(8,128)(2,1)S(1)} collective-permute-done((bf16[256,256]{1,0:T(8,128)(2,1)S(1)}, bf16[256,256]{1,0:T(8,128)(2,1)S(1)}, u32[]{:S(2)}, u32[]{:S(2)}) %collective-permute-start.15) | collective-permute-done | bytes 131104 | tf_op jit(solution)/shard_map/ppermute | solution.py:29
  139.4 3.3 %down_product.2 = bf16[256,1792]{1,0:T(8,128)(2,1)S(1)} custom-call(bf16[256,256]{1,0:T(8,128)(2,1)S(1)} %hidden_units.2.refs_0_, bf16[256,256]{1,0:T(8,128)(2,1)S(1)} %collective-permute-done.13.refs_1_, bf16[256,256]{1,0:T(8,128)(2,1)S(1)} %collective-permute-done.14.refs_2_, bf16[256,256]{1,0:T(8,128)(2,1)S(1)} %collective-permute-done.15.refs_3_, ...), custom_call_target="tpu_custom_call" | custom-call | flops 939524096 | bytes 3670016 | tf_op jit(solution)/shard_map/down_product/pallas_call | solution.py:149
  145.3 8.3 %all-to-all-start.3 = ((bf16[32,8,1792]{2,1,0:T(8,128)(2,1)}), bf16[32,8,1792]{2,1,0:T(8,128)(2,1)}, u32[]{:S(2)}, u32[]{:S(2)}) async-start(bf16[32,8,1792]{2,1,0:T(8,128)(2,1)} %bitcast.90), calls=%async_computation.3 | async-start | bytes 1835008 | tf_op jit(solution)/shard_map/all_to_all | solution.py:39
  157.9 3.5 %near_sums.3.sums = f32[256,512]{1,0:T(8,128)S(1)} custom-call(bf16[256,1792]{1,0:T(8,128)(2,1)} %get-tuple-element.49.own, bf16[256,1792]{1,0:T(8,128)(2,1)} %collective-permute-done.16.below, bf16[256,1792]{1,0:T(8,128)(2,1)} %collective-permute-done.17.above, bf16[1792,256]{1,0:T(8,128)(2,1)S(1)} %copy-done.4, bf16[1792,256]{1,0:T(8,128)(2,1)S(1)} %copy-done.2, ...), custom_call_target="tpu_custom_call" | custom-call | flops 1409286144 | bytes 5505024 | tf_op jit(solution)/shard_map/near_sums/pallas_call | solution.py:89
  165.1 2.7 %collective-permute-done.20.refs_1_ = bf16[256,256]{1,0:T(8,128)(2,1)S(1)} collective-permute-done((bf16[256,256]{1,0:T(8,128)(2,1)S(1)}, bf16[256,256]{1,0:T(8,128)(2,1)S(1)}, u32[]{:S(2)}, u32[]{:S(2)}) %collective-permute-start.20) | collective-permute-done | bytes 131104 | tf_op jit(solution)/shard_map/ppermute | solution.py:29
  170.7 4.3 %down_product.3 = bf16[256,1792]{1,0:T(8,128)(2,1)} custom-call(bf16[256,256]{1,0:T(8,128)(2,1)S(1)} %hidden_units.3.refs_0_, bf16[256,256]{1,0:T(8,128)(2,1)S(1)} %collective-permute-done.20.refs_1_, bf16[256,256]{1,0:T(8,128)(2,1)S(1)} %collective-permute-done.21.refs_2_, bf16[256,256]{1,0:T(8,128)(2,1)S(1)} %collective-permute-done.22.refs_3_, ...), custom_call_target="tpu_custom_call" | custom-call | flops 939524096 | bytes 3670016 | tf_op jit(solution)/shard_map/down_product/pallas_call | solution.py:149
  175.0 9.1 %all-to-all-start.2 = ((bf16[32,8,1792]{2,1,0:T(8,128)(2,1)}), bf16[32,8,1792]{2,1,0:T(8,128)(2,1)S(1)}, u32[]{:S(2)}, u32[]{:S(2)}) async-start(bf16[32,8,1792]{2,1,0:T(8,128)(2,1)} %bitcast.28), calls=%async_computation.2 | async-start | bytes 1835008 | tf_op jit(solution)/shard_map/all_to_all | solution.py:39
  191.2 9.7 %all-to-all-done.2 = bf16[32,8,1792]{2,1,0:T(8,128)(2,1)S(1)} async-done(((bf16[32,8,1792]{2,1,0:T(8,128)(2,1)}), bf16[32,8,1792]{2,1,0:T(8,128)(2,1)S(1)}, u32[]{:S(2)}, u32[]{:S(2)}) %all-to-all-start.2) | async-done | bytes 917536 | tf_op jit(solution)/shard_map/all_to_all | solution.py:39
  201.6 9.9 %collective-permute-start.23 = (bf16[32,1792]{1,0:T(8,128)(2,1)S(1)}, bf16[32,1792]{1,0:T(8,128)(2,1)S(1)}, u32[]{:S(2)}, u32[]{:S(2)}) collective-permute-start(bf16[32,1792]{1,0:T(8,128)(2,1)S(1)} %slice.130), channel_id=1, source_target_pairs={{0,2},{2,0},{4,6},{6,4},{8,10},{10,8},{12,14},{14,12},{16,18},{18,... | collective-permute-start | bytes 344072 | tf_op jit(solution)/shard_map/ppermute | solution.py:33
  (236 shorter events, 74.9 us)
Async XLA Ops:
  12.4 57.9 %all-to-all-start = ((bf16[32,16,1792]{2,1,0:T(8,128)(2,1)}), bf16[32,16,1792]{2,1,0:T(8,128)(2,1)}, u32[]{:S(2)}, u32[]{:S(2)}) async-start(bf16[32,16,1792]{2,1,0:T(8,128)(2,1)} %bitcast.7), calls=%async_computation | async-start | bytes 3670016 | tf_op jit(solution)/shard_map/all_to_all | solution.py:39
  26.0 36.3 %collective-permute-start.2 = (bf16[256,1792]{1,0:T(8,128)(2,1)}, bf16[256,1792]{1,0:T(8,128)(2,1)S(1)}, u32[]{:S(2)}, u32[]{:S(2)}) collective-permute-start(bf16[256,1792]{1,0:T(8,128)(2,1)} %get-tuple-element.75), channel_id=1, source_target_pairs={{0,128},{128,1},{1,129},{129,0},{2,130},{130,3},{3,131},{131,2},{4... | collective-permute-start | bytes 2752520 | tf_op jit(solution)/shard_map/ppermute | solution.py:29
  27.3 35.0 %collective-permute-start.3 = (bf16[256,1792]{1,0:T(8,128)(2,1)}, bf16[256,1792]{1,0:T(8,128)(2,1)S(1)}, u32[]{:S(2)}, u32[]{:S(2)}) collective-permute-start(bf16[256,1792]{1,0:T(8,128)(2,1)} %get-tuple-element.77), channel_id=1, source_target_pairs={{0,129},{128,0},{1,128},{129,1},{2,131},{130,2},{3,130},{131,3},{4... | collective-permute-start | bytes 2752520 | tf_op jit(solution)/shard_map/ppermute | solution.py:29
  29.5 19.0 %collective-permute-start.8 = (f32[64]{0:T(128)}, f32[64]{0:T(128)S(1)}, u32[]{:S(2)}, u32[]{:S(2)}) collective-permute-start(f32[64]{0:T(128)} %maximum_bitcast_fusion), channel_id=1, source_target_pairs={{0,129},{128,0},{1,128},{129,1},{2,131},{130,2},{3,130},{131,3},{4... | collective-permute-start | bytes 776 | tf_op jit(solution)/shard_map/ppermute | solution.py:29
  31.7 19.4 %collective-permute-start.7 = (f32[64]{0:T(128)}, f32[64]{0:T(128)}, u32[]{:S(2)}, u32[]{:S(2)}) collective-permute-start(f32[64]{0:T(128)} %maximum_bitcast_fusion), channel_id=1, source_target_pairs={{0,1},{128,129},{1,0},{129,128},{2,3},{130,131},{3,2},{131,130},{4... | collective-permute-start | bytes 776 | tf_op jit(solution)/shard_map/ppermute | solution.py:29
  32.7 20.6 %collective-permute-start.6 = (f32[64]{0:T(128)}, f32[64]{0:T(128)S(1)}, u32[]{:S(2)}, u32[]{:S(2)}) collective-permute-start(f32[64]{0:T(128)} %maximum_bitcast_fusion), channel_id=1, source_target_pairs={{0,128},{128,1},{1,129},{129,0},{2,130},{130,3},{3,131},{131,2},{4... | collective-permute-start | bytes 776 | tf_op jit(solution)/shard_map/ppermute | solution.py:29
  48.5 21.8 %collective-permute-start.4 = (bf16[256,1792]{1,0:T(8,128)(2,1)}, bf16[256,1792]{1,0:T(8,128)(2,1)}, u32[]{:S(2)}, u32[]{:S(2)}) collective-permute-start(bf16[256,1792]{1,0:T(8,128)(2,1)} %get-tuple-element.74), channel_id=1, source_target_pairs={{0,1},{128,129},{1,0},{129,128},{2,3},{130,131},{3,2},{131,130},{4... | collective-permute-start | bytes 2752520 | tf_op jit(solution)/shard_map/ppermute | solution.py:29
  73.1 20.8 %collective-permute-start.9 = (bf16[256,1792]{1,0:T(8,128)(2,1)}, bf16[256,1792]{1,0:T(8,128)(2,1)}, u32[]{:S(2)}, u32[]{:S(2)}) collective-permute-start(bf16[256,1792]{1,0:T(8,128)(2,1)} %get-tuple-element.79.own), channel_id=1, source_target_pairs={{0,128},{128,1},{1,129},{129,0},{2,130},{130,3},{3,131},{131,2},{4... | collective-permute-start | bytes 2752520 | tf_op jit(solution)/shard_map/ppermute | solution.py:29
  74.3 19.6 %collective-permute-start.10 = (bf16[256,1792]{1,0:T(8,128)(2,1)}, bf16[256,1792]{1,0:T(8,128)(2,1)}, u32[]{:S(2)}, u32[]{:S(2)}) collective-permute-start(bf16[256,1792]{1,0:T(8,128)(2,1)} %get-tuple-element.79.own), channel_id=1, source_target_pairs={{0,129},{128,0},{1,128},{129,1},{2,131},{130,2},{3,130},{131,3},{4... | collective-permute-start | bytes 2752520 | tf_op jit(solution)/shard_map/ppermute | solution.py:29
  76.1 29.5 %all-to-all-start.1 = ((bf16[32,8,640]{2,1,0:T(8,128)(2,1)}), bf16[32,8,640]{2,1,0:T(8,128)(2,1)S(1)}, u32[]{:S(2)}, u32[]{:S(2)}) async-start(bf16[32,8,640]{2,1,0:T(8,128)(2,1)} %bitcast.99), calls=%async_computation.1 | async-start | bytes 655360 | tf_op jit(solution)/shard_map/all_to_all | solution.py:39
  93.9 20.7 %collective-permute-start.16 = (bf16[256,1792]{1,0:T(8,128)(2,1)}, bf16[256,1792]{1,0:T(8,128)(2,1)}, u32[]{:S(2)}, u32[]{:S(2)}) collective-permute-start(bf16[256,1792]{1,0:T(8,128)(2,1)} %get-tuple-element.49.own), channel_id=1, source_target_pairs={{0,128},{128,1},{1,129},{129,0},{2,130},{130,3},{3,131},{131,2},{4... | collective-permute-start | bytes 2752520 | tf_op jit(solution)/shard_map/ppermute | solution.py:29
  94.4 21.4 %collective-permute-start.17 = (bf16[256,1792]{1,0:T(8,128)(2,1)}, bf16[256,1792]{1,0:T(8,128)(2,1)}, u32[]{:S(2)}, u32[]{:S(2)}) collective-permute-start(bf16[256,1792]{1,0:T(8,128)(2,1)} %get-tuple-element.49.own), channel_id=1, source_target_pairs={{0,129},{128,0},{1,128},{129,1},{2,131},{130,2},{3,130},{131,3},{4... | collective-permute-start | bytes 2752520 | tf_op jit(solution)/shard_map/ppermute | solution.py:29
  99.9 23.6 %collective-permute-start.11 = (bf16[128,1792]{1,0:T(8,128)(2,1)}, bf16[128,1792]{1,0:T(8,128)(2,1)}, u32[]{:S(2)}, u32[]{:S(2)}) collective-permute-start(bf16[128,1792]{1,0:T(8,128)(2,1)} %slice.76), channel_id=1, source_target_pairs={{0,128},{128,1},{1,129},{129,0},{2,130},{130,3},{3,131},{131,2},{4... | collective-permute-start | bytes 1376264 | tf_op jit(solution)/shard_map/ppermute | solution.py:29
  101.7 21.8 %collective-permute-start.12 = (bf16[128,1792]{1,0:T(8,128)(2,1)}, bf16[128,1792]{1,0:T(8,128)(2,1)}, u32[]{:S(2)}, u32[]{:S(2)}) collective-permute-start(bf16[128,1792]{1,0:T(8,128)(2,1)} %slice.77), channel_id=1, source_target_pairs={{0,129},{128,0},{1,128},{129,1},{2,131},{130,2},{3,130},{131,3},{4... | collective-permute-start | bytes 1376264 | tf_op jit(solution)/shard_map/ppermute | solution.py:29
  115.7 28.0 %collective-permute-start.18 = (bf16[128,1792]{1,0:T(8,128)(2,1)S(1)}, bf16[128,1792]{1,0:T(8,128)(2,1)S(1)}, u32[]{:S(2)}, u32[]{:S(2)}) collective-permute-start(bf16[128,1792]{1,0:T(8,128)(2,1)S(1)} %slice.95), channel_id=1, source_target_pairs={{0,128},{128,1},{1,129},{129,0},{2,130},{130,3},{3,131},{131,2},{4... | collective-permute-start | bytes 1376264 | tf_op jit(solution)/shard_map/ppermute | solution.py:29
  116.9 27.6 %collective-permute-start.19 = (bf16[128,1792]{1,0:T(8,128)(2,1)S(1)}, bf16[128,1792]{1,0:T(8,128)(2,1)S(1)}, u32[]{:S(2)}, u32[]{:S(2)}) collective-permute-start(bf16[128,1792]{1,0:T(8,128)(2,1)S(1)} %slice.96), channel_id=1, source_target_pairs={{0,129},{128,0},{1,128},{129,1},{2,131},{130,2},{3,130},{131,3},{4... | collective-permute-start | bytes 1376264 | tf_op jit(solution)/shard_map/ppermute | solution.py:29
  125.3 10.7 %collective-permute-start.13 = (bf16[256,256]{1,0:T(8,128)(2,1)S(1)}, bf16[256,256]{1,0:T(8,128)(2,1)S(1)}, u32[]{:S(2)}, u32[]{:S(2)}) collective-permute-start(bf16[256,256]{1,0:T(8,128)(2,1)S(1)} %hidden_units.2.refs_0_), channel_id=1, source_target_pairs={{0,128},{128,1},{1,129},{129,0},{2,130},{130,3},{3,131},{131,2},{4... | collective-permute-start | bytes 393224 | tf_op jit(solution)/shard_map/ppermute | solution.py:29
  125.6 10.4 %collective-permute-start.14 = (bf16[256,256]{1,0:T(8,128)(2,1)S(1)}, bf16[256,256]{1,0:T(8,128)(2,1)S(1)}, u32[]{:S(2)}, u32[]{:S(2)}) collective-permute-start(bf16[256,256]{1,0:T(8,128)(2,1)S(1)} %hidden_units.2.refs_0_), channel_id=1, source_target_pairs={{0,129},{128,0},{1,128},{129,1},{2,131},{130,2},{3,130},{131,3},{4... | collective-permute-start | bytes 393224 | tf_op jit(solution)/shard_map/ppermute | solution.py:29
  128.1 11.3 %collective-permute-start.15 = (bf16[256,256]{1,0:T(8,128)(2,1)S(1)}, bf16[256,256]{1,0:T(8,128)(2,1)S(1)}, u32[]{:S(2)}, u32[]{:S(2)}) collective-permute-start(bf16[256,256]{1,0:T(8,128)(2,1)S(1)} %hidden_units.2.refs_0_), channel_id=1, source_target_pairs={{0,1},{128,129},{1,0},{129,128},{2,3},{130,131},{3,2},{131,130},{4... | collective-permute-start | bytes 393224 | tf_op jit(solution)/shard_map/ppermute | solution.py:29
  145.3 29.7 %all-to-all-start.3 = ((bf16[32,8,1792]{2,1,0:T(8,128)(2,1)}), bf16[32,8,1792]{2,1,0:T(8,128)(2,1)}, u32[]{:S(2)}, u32[]{:S(2)}) async-start(bf16[32,8,1792]{2,1,0:T(8,128)(2,1)} %bitcast.90), calls=%async_computation.3 | async-start | bytes 1835008 | tf_op jit(solution)/shard_map/all_to_all | solution.py:39
  162.2 5.5 %collective-permute-start.20 = (bf16[256,256]{1,0:T(8,128)(2,1)S(1)}, bf16[256,256]{1,0:T(8,128)(2,1)S(1)}, u32[]{:S(2)}, u32[]{:S(2)}) collective-permute-start(bf16[256,256]{1,0:T(8,128)(2,1)S(1)} %hidden_units.3.refs_0_), channel_id=1, source_target_pairs={{0,128},{128,1},{1,129},{129,0},{2,130},{130,3},{3,131},{131,2},{4... | collective-permute-start | bytes 393224 | tf_op jit(solution)/shard_map/ppermute | solution.py:29
  165.0 5.7 %collective-permute-start.22 = (bf16[256,256]{1,0:T(8,128)(2,1)S(1)}, bf16[256,256]{1,0:T(8,128)(2,1)S(1)}, u32[]{:S(2)}, u32[]{:S(2)}) collective-permute-start(bf16[256,256]{1,0:T(8,128)(2,1)S(1)} %hidden_units.3.refs_0_), channel_id=1, source_target_pairs={{0,1},{128,129},{1,0},{129,128},{2,3},{130,131},{3,2},{131,130},{4... | collective-permute-start | bytes 393224 | tf_op jit(solution)/shard_map/ppermute | solution.py:29
  175.0 25.9 %all-to-all-start.2 = ((bf16[32,8,1792]{2,1,0:T(8,128)(2,1)}), bf16[32,8,1792]{2,1,0:T(8,128)(2,1)S(1)}, u32[]{:S(2)}, u32[]{:S(2)}) async-start(bf16[32,8,1792]{2,1,0:T(8,128)(2,1)} %bitcast.28), calls=%async_computation.2 | async-start | bytes 1835008 | tf_op jit(solution)/shard_map/all_to_all | solution.py:39
  201.6 10.8 %collective-permute-start.23 = (bf16[32,1792]{1,0:T(8,128)(2,1)S(1)}, bf16[32,1792]{1,0:T(8,128)(2,1)S(1)}, u32[]{:S(2)}, u32[]{:S(2)}) collective-permute-start(bf16[32,1792]{1,0:T(8,128)(2,1)S(1)} %slice.130), channel_id=1, source_target_pairs={{0,2},{2,0},{4,6},{6,4},{8,10},{10,8},{12,14},{14,12},{16,18},{18,... | collective-permute-start | bytes 344072 | tf_op jit(solution)/shard_map/ppermute | solution.py:33
  (62 other events, 625.6 us)

commit v2 on v1

--- a/solution.py
+++ b/solution.py
@@ -300,7 +300,6 @@
     near = [neighbours(arrived[0])]
     near[0], arrived[1], blocks = lax.optimization_barrier((near[0], arrived[1], blocks))
     near.append(neighbours(arrived[1]))
-    far = [across(*v) for v in near]
 
     weight = meta[:, topk : 2 * topk]
     share = weight / jnp.sum(weight, axis=1, keepdims=True)
@@ -314,13 +313,13 @@
     contract = (((0,), (0,)), ((), ()))
     for c in range(CHUNKS):
         below, above = near[c]
-        low, high = far[c]
+        low, high = across(below, above)
         sums = near_sums(arrived[c], below, above, blocks[:6])
         hidden = hidden_units(low, high, sums, factors[c], *blocks[6:])
         hidden = [over_y(hidden, k) for k in ORDER]
         out = down_product(hidden, downs)
         if c == 0:
-            out, near[1], far[1] = lax.optimization_barrier((out, near[1], far[1]))
+            out, near[1] = lax.optimization_barrier((out, near[1]))
         back = exchange(out).reshape(n, -1)
         if c == 1:
             back, attn_out, mixed, mixes = lax.optimization_barrier((back, attn_out, mixed, mixes))

time: 215 us -> 221 us (1.028)
  waiting for transfers between devices: 56.9 us -> 52.7 us
  local copies, waits for them, and re-layouts: 33.3 us -> 37.1 us
  other arithmetic: 10.9 us -> 14.3 us
    ppermute x20, waiting for transfers between devices: 46.2 us -> 42.9 us  [over_y(): return lax.ppermute(v, GROUP, y_perm(k % NY)) if k % NY else v]
    unnamed x116 -> x124, local copies, waits for them, and re-layouts: 9.04 us -> 11.4 us
  transfers between devices with their start and end apart: 28 -> 28, of which waited for: 11 -> 11; matrix products, arithmetic and copies ran while one was open for 20% -> 22% of each run, Pallas kernels for 8% -> 8%
where the time goes in v2:
time: 221 us; the launch traced here: 220 us
  starting transfers between devices  77.6 us (35%)
  waiting for transfers between devices  52.7 us (24%)
  local copies, waits for them, and re-layouts  37.1 us (17%)
  Pallas kernels  18.3 us (8%)
  matrix products  18 us (8%)
  other arithmetic  14.3 us (6%)
    ppermute x20, waiting for transfers between devices, over_y(): return lax.ppermute(v, GROUP, y_perm(k % NY)) if k % NY else v  42.9 us
    all_to_all x4, starting transfers between devices, chips_exchange(): lax.all_to_all(v, 'ep', split_axis=0, concat_axis=0, tiled=True, axis_ind...  35.7 us
    ppermute x20, starting transfers between devices, over_y(): return lax.ppermute(v, GROUP, y_perm(k % NY)) if k % NY else v  25.2 us
    ppermute x4, starting transfers between devices, other_core(): lax.ppermute(v, 'ep', [(i, i ^ 1) for i in range(lax.axis_size('ep'))])  16.7 us
    unnamed x124, local copies, waits for them, and re-layouts  11.4 us
    all_to_all x4, waiting for transfers between devices, chips_exchange(): lax.all_to_all(v, 'ep', split_axis=0, concat_axis=0, tiled=True, axis_ind...  8.9 us
    pallas_call x2, Pallas kernels, down_product(): pl.pallas_call(lambda *refs: down_kernel(len(hidden), len(downs), *refs),...  7.63 us
    slice x4, local copies, waits for them, and re-layouts, across(): return (over_y(below[:mid], 1), over_y(above[mid:], -1))  7.28 us
  transfers between devices with their start and end apart: 28, of which 11 were waited for; matrix products, arithmetic and copies ran while one was open for 22% of the time, Pallas kernels for 8%

profile of v2, /device:TPU:1, one launch (start us, length us, event | category | flops | bytes accessed | tf_op | source)
XLA Modules:
  0.0 219.7 jit_solution(8640275438123884049)
XLA Ops:
  3.5 3.3 %collective-permute-start = (f32[32,17]{0,1:T(8,128)S(1)}, f32[32,17]{0,1:T(8,128)S(1)}, u32[]{:S(2)}, u32[]{:S(2)}) collective-permute-start(f32[32,17]{0,1:T(8,128)S(1)} %pad_maximum_fusion.2), channel_id=1, source_target_pairs={{0,2},{2,0},{4,6},{6,4},{8,10},{10,8},{12,14},{14,12},{16,18},{18,... | collective-permute-start | bytes 6536 | tf_op jit(solution)/shard_map/ppermute | solution.py:33
  12.4 9.4 %all-to-all-start = ((bf16[32,16,1792]{2,1,0:T(8,128)(2,1)}), bf16[32,16,1792]{2,1,0:T(8,128)(2,1)}, u32[]{:S(2)}, u32[]{:S(2)}) async-start(bf16[32,16,1792]{2,1,0:T(8,128)(2,1)} %bitcast.7), calls=%async_computation | async-start | bytes 3670016 | tf_op jit(solution)/shard_map/all_to_all | solution.py:39
  22.1 4.0 %dynamic-slice_bitcast_fusion = (bf16[256,1792]{1,0:T(8,128)(2,1)}, bf16[256,1792]{1,0:T(8,128)(2,1)}, bf16[256,1792]{1,0:T(8,128)(2,1)}, bf16[256,1792]{1,0:T(8,128)(2,1)}) fusion(bf16[1,256,7168]{2,1,0:T(8,128)(2,1)} %param.27, s32[]{:T(128)S(6)} %select_n.258, s32[]{:T(128)S(6)} %select_n.248, s32[]{:T(128)S(6)} %select_n.243, s32[]{:T(128)S(6)} %select_n.253), kind=kLoop, calls=%fused_computation.24 | loop fusion | bytes 7340048 | tf_op jit(solution)/shard_map/dynamic_slice | solution.py:245
  34.2 14.3 %collective-permute-done.8 = f32[64]{0:T(128)S(1)} collective-permute-done((f32[64]{0:T(128)S(1)}, f32[64]{0:T(128)S(1)}, u32[]{:S(2)}, u32[]{:S(2)}) %collective-permute-start.8) | collective-permute-done | bytes 288 | tf_op jit(solution)/shard_map/ppermute | solution.py:29
  48.5 2.6 %collective-permute-start.4 = (bf16[256,1792]{1,0:T(8,128)(2,1)}, bf16[256,1792]{1,0:T(8,128)(2,1)}, u32[]{:S(2)}, u32[]{:S(2)}) collective-permute-start(bf16[256,1792]{1,0:T(8,128)(2,1)} %get-tuple-element.70), channel_id=1, source_target_pairs={{0,1},{128,129},{1,0},{129,128},{2,3},{130,131},{3,2},{131,130},{4... | collective-permute-start | bytes 2752520 | tf_op jit(solution)/shard_map/ppermute | solution.py:29
  62.3 8.0 %collective-permute-done.4.refs_7_ = bf16[256,1792]{1,0:T(8,128)(2,1)} collective-permute-done((bf16[256,1792]{1,0:T(8,128)(2,1)}, bf16[256,1792]{1,0:T(8,128)(2,1)}, u32[]{:S(2)}, u32[]{:S(2)}) %collective-permute-start.4) | collective-permute-done | bytes 917536 | tf_op jit(solution)/shard_map/ppermute | solution.py:29
  70.3 2.9 %slice_bitcast_fusion = (bf16[256,1792]{1,0:T(8,128)(2,1)}, bf16[256,1792]{1,0:T(8,128)(2,1)}) fusion(bf16[32,16,1792]{2,1,0:T(8,128)(2,1)} %all-to-all-done), kind=kLoop, calls=%fused_computation.22 | loop fusion | bytes 3670016 | tf_op jit(solution)/shard_map/reshape | solution.py:290
  78.2 8.7 %all-to-all-start.1 = ((bf16[32,8,640]{2,1,0:T(8,128)(2,1)}), bf16[32,8,640]{2,1,0:T(8,128)(2,1)S(1)}, u32[]{:S(2)}, u32[]{:S(2)}) async-start(bf16[32,8,640]{2,1,0:T(8,128)(2,1)} %bitcast.24), calls=%async_computation.1 | async-start | bytes 655360 | tf_op jit(solution)/shard_map/all_to_all | solution.py:39
  86.9 5.6 %constant_dynamic-slice_fusion = (bf16[1792,256]{1,0:T(8,128)(2,1)}, bf16[1792,256]{1,0:T(8,128)(2,1)S(1)}, bf16[1792,256]{1,0:T(8,128)(2,1)S(1)}, bf16[1792,256...) fusion(bf16[7168,256]{1,0:T(8,128)(2,1)} %bitcast.93, ...), kind=kLoop, calls=%fused_computation.103 | loop fusion | bytes 14680080 | tf_op jit(solution)/shard_map/dynamic_slice | solution.py:285
  100.3 2.7 %collective-permute-start.12 = (bf16[128,1792]{1,0:T(8,128)(2,1)}, bf16[128,1792]{1,0:T(8,128)(2,1)}, u32[]{:S(2)}, u32[]{:S(2)}) collective-permute-start(bf16[128,1792]{1,0:T(8,128)(2,1)} %slice.77), channel_id=1, source_target_pairs={{0,129},{128,0},{1,128},{129,1},{2,131},{130,2},{3,130},{131,3},{4... | collective-permute-start | bytes 1376264 | tf_op jit(solution)/shard_map/ppermute | solution.py:29
  109.9 3.4 %near_sums.2.sums = f32[256,512]{1,0:T(8,128)S(1)} custom-call(bf16[256,1792]{1,0:T(8,128)(2,1)} %get-tuple-element.75.own, bf16[256,1792]{1,0:T(8,128)(2,1)} %collective-permute-done.9.below, bf16[256,1792]{1,0:T(8,128)(2,1)} %collective-permute-done.10.above, bf16[1792,256]{1,0:T(8,128)(2,1)S(1)} %copy-done.3, bf16[1792,256]{1,0:T(8,128)(2,1)S(1)} %copy-done.1, ...), custom_call_target="tpu_custom_call" | custom-call | flops 1409286144 | bytes 5505024 | tf_op jit(solution)/shard_map/near_sums/pallas_call | solution.py:89
  113.4 10.2 %collective-permute-done.11.low = bf16[128,1792]{1,0:T(8,128)(2,1)} collective-permute-done((bf16[128,1792]{1,0:T(8,128)(2,1)}, bf16[128,1792]{1,0:T(8,128)(2,1)}, u32[]{:S(2)}, u32[]{:S(2)}) %collective-permute-start.11) | collective-permute-done | bytes 458784 | tf_op jit(solution)/shard_map/ppermute | solution.py:29
  125.7 2.5 %collective-permute-start.14 = (bf16[256,256]{1,0:T(8,128)(2,1)S(1)}, bf16[256,256]{1,0:T(8,128)(2,1)S(1)}, u32[]{:S(2)}, u32[]{:S(2)}) collective-permute-start(bf16[256,256]{1,0:T(8,128)(2,1)S(1)} %hidden_units.2.refs_0_), channel_id=1, source_target_pairs={{0,129},{128,0},{1,128},{129,1},{2,131},{130,2},{3,130},{131,3},{4... | collective-permute-start | bytes 393224 | tf_op jit(solution)/shard_map/ppermute | solution.py:29
  130.5 3.0 %collective-permute-done.15.refs_3_ = bf16[256,256]{1,0:T(8,128)(2,1)S(1)} collective-permute-done((bf16[256,256]{1,0:T(8,128)(2,1)S(1)}, bf16[256,256]{1,0:T(8,128)(2,1)S(1)}, u32[]{:S(2)}, u32[]{:S(2)}) %collective-permute-start.15) | collective-permute-done | bytes 131104 | tf_op jit(solution)/shard_map/ppermute | solution.py:29
  133.5 3.3 %down_product.2 = bf16[256,1792]{1,0:T(8,128)(2,1)S(1)} custom-call(bf16[256,256]{1,0:T(8,128)(2,1)S(1)} %hidden_units.2.refs_0_, bf16[256,256]{1,0:T(8,128)(2,1)S(1)} %collective-permute-done.13.refs_1_, bf16[256,256]{1,0:T(8,128)(2,1)S(1)} %collective-permute-done.14.refs_2_, bf16[256,256]{1,0:T(8,128)(2,1)S(1)} %collective-permute-done.15.refs_3_, ...), custom_call_target="tpu_custom_call" | custom-call | flops 939524096 | bytes 3670016 | tf_op jit(solution)/shard_map/down_product/pallas_call | solution.py:149
  137.8 8.2 %all-to-all-start.3 = ((bf16[32,8,1792]{2,1,0:T(8,128)(2,1)}), bf16[32,8,1792]{2,1,0:T(8,128)(2,1)}, u32[]{:S(2)}, u32[]{:S(2)}) async-start(bf16[32,8,1792]{2,1,0:T(8,128)(2,1)} %bitcast.90), calls=%async_computation.3 | async-start | bytes 1835008 | tf_op jit(solution)/shard_map/all_to_all | solution.py:39
  154.2 2.5 %collective-permute-start.19 = (bf16[128,1792]{1,0:T(8,128)(2,1)}, bf16[128,1792]{1,0:T(8,128)(2,1)}, u32[]{:S(2)}, u32[]{:S(2)}) collective-permute-start(bf16[128,1792]{1,0:T(8,128)(2,1)} %slice.80), channel_id=1, source_target_pairs={{0,129},{128,0},{1,128},{129,1},{2,131},{130,2},{3,130},{131,3},{4... | collective-permute-start | bytes 1376264 | tf_op jit(solution)/shard_map/ppermute | solution.py:29
  163.0 3.4 %near_sums.3.sums = f32[256,512]{1,0:T(8,128)S(1)} custom-call(bf16[256,1792]{1,0:T(8,128)(2,1)} %get-tuple-element.47.own, bf16[256,1792]{1,0:T(8,128)(2,1)} %collective-permute-done.16.below, bf16[256,1792]{1,0:T(8,128)(2,1)} %collective-permute-done.17.above, bf16[1792,256]{1,0:T(8,128)(2,1)S(1)} %copy-done.4, bf16[1792,256]{1,0:T(8,128)(2,1)S(1)} %copy-done.2, ...), custom_call_target="tpu_custom_call" | custom-call | flops 1409286144 | bytes 5505024 | tf_op jit(solution)/shard_map/near_sums/pallas_call | solution.py:89
  168.6 2.7 %collective-permute-start.21 = (bf16[256,256]{1,0:T(8,128)(2,1)S(1)}, bf16[256,256]{1,0:T(8,128)(2,1)S(1)}, u32[]{:S(2)}, u32[]{:S(2)}) collective-permute-start(bf16[256,256]{1,0:T(8,128)(2,1)S(1)} %hidden_units.3.refs_0_), channel_id=1, source_target_pairs={{0,129},{128,0},{1,128},{129,1},{2,131},{130,2},{3,130},{131,3},{4... | collective-permute-start | bytes 393224 | tf_op jit(solution)/shard_map/ppermute | solution.py:29
  171.3 2.3 %collective-permute-done.20.refs_1_ = bf16[256,256]{1,0:T(8,128)(2,1)S(1)} collective-permute-done((bf16[256,256]{1,0:T(8,128)(2,1)S(1)}, bf16[256,256]{1,0:T(8,128)(2,1)S(1)}, u32[]{:S(2)}, u32[]{:S(2)}) %collective-permute-start.20) | collective-permute-done | bytes 131104 | tf_op jit(solution)/shard_map/ppermute | solution.py:29
  176.6 4.3 %down_product.3 = bf16[256,1792]{1,0:T(8,128)(2,1)} custom-call(bf16[256,256]{1,0:T(8,128)(2,1)S(1)} %hidden_units.3.refs_0_, bf16[256,256]{1,0:T(8,128)(2,1)S(1)} %collective-permute-done.20.refs_1_, bf16[256,256]{1,0:T(8,128)(2,1)S(1)} %collective-permute-done.21.refs_2_, bf16[256,256]{1,0:T(8,128)(2,1)S(1)} %collective-permute-done.22.refs_3_, ...), custom_call_target="tpu_custom_call" | custom-call | flops 939524096 | bytes 3670016 | tf_op jit(solution)/shard_map/down_product/pallas_call | solution.py:149
  180.9 9.3 %all-to-all-start.2 = ((bf16[32,8,1792]{2,1,0:T(8,128)(2,1)}), bf16[32,8,1792]{2,1,0:T(8,128)(2,1)S(1)}, u32[]{:S(2)}, u32[]{:S(2)}) async-start(bf16[32,8,1792]{2,1,0:T(8,128)(2,1)} %bitcast.28), calls=%async_computation.2 | async-start | bytes 1835008 | tf_op jit(solution)/shard_map/all_to_all | solution.py:39
  197.4 8.9 %all-to-all-done.2 = bf16[32,8,1792]{2,1,0:T(8,128)(2,1)S(1)} async-done(((bf16[32,8,1792]{2,1,0:T(8,128)(2,1)}), bf16[32,8,1792]{2,1,0:T(8,128)(2,1)S(1)}, u32[]{:S(2)}, u32[]{:S(2)}) %all-to-all-start.2) | async-done | bytes 917536 | tf_op jit(solution)/shard_map/all_to_all | solution.py:39
  206.9 11.1 %collective-permute-start.23 = (bf16[32,1792]{1,0:T(8,128)(2,1)S(1)}, bf16[32,1792]{1,0:T(8,128)(2,1)S(1)}, u32[]{:S(2)}, u32[]{:S(2)}) collective-permute-start(bf16[32,1792]{1,0:T(8,128)(2,1)S(1)} %slice.128), channel_id=1, source_target_pairs={{0,2},{2,0},{4,6},{6,4},{8,10},{10,8},{12,14},{14,12},{16,18},{18,... | collective-permute-start | bytes 344072 | tf_op jit(solution)/shard_map/ppermute | solution.py:33
  (244 shorter events, 81.4 us)
Async XLA Ops:
  3.5 5.1 %collective-permute-start = (f32[32,17]{0,1:T(8,128)S(1)}, f32[32,17]{0,1:T(8,128)S(1)}, u32[]{:S(2)}, u32[]{:S(2)}) collective-permute-start(f32[32,17]{0,1:T(8,128)S(1)} %pad_maximum_fusion.2), channel_id=1, source_target_pairs={{0,2},{2,0},{4,6},{6,4},{8,10},{10,8},{12,14},{14,12},{16,18},{18,... | collective-permute-start | bytes 6536 | tf_op jit(solution)/shard_map/ppermute | solution.py:33
  12.4 57.9 %all-to-all-start = ((bf16[32,16,1792]{2,1,0:T(8,128)(2,1)}), bf16[32,16,1792]{2,1,0:T(8,128)(2,1)}, u32[]{:S(2)}, u32[]{:S(2)}) async-start(bf16[32,16,1792]{2,1,0:T(8,128)(2,1)} %bitcast.7), calls=%async_computation | async-start | bytes 3670016 | tf_op jit(solution)/shard_map/all_to_all | solution.py:39
  26.1 36.2 %collective-permute-start.2 = (bf16[256,1792]{1,0:T(8,128)(2,1)}, bf16[256,1792]{1,0:T(8,128)(2,1)S(1)}, u32[]{:S(2)}, u32[]{:S(2)}) collective-permute-start(bf16[256,1792]{1,0:T(8,128)(2,1)} %get-tuple-element.71), channel_id=1, source_target_pairs={{0,128},{128,1},{1,129},{129,0},{2,130},{130,3},{3,131},{131,2},{4... | collective-permute-start | bytes 2752520 | tf_op jit(solution)/shard_map/ppermute | solution.py:29
  27.4 34.9 %collective-permute-start.3 = (bf16[256,1792]{1,0:T(8,128)(2,1)}, bf16[256,1792]{1,0:T(8,128)(2,1)S(1)}, u32[]{:S(2)}, u32[]{:S(2)}) collective-permute-start(bf16[256,1792]{1,0:T(8,128)(2,1)} %get-tuple-element.73), channel_id=1, source_target_pairs={{0,129},{128,0},{1,128},{129,1},{2,131},{130,2},{3,130},{131,3},{4... | collective-permute-start | bytes 2752520 | tf_op jit(solution)/shard_map/ppermute | solution.py:29
  30.4 18.1 %collective-permute-start.8 = (f32[64]{0:T(128)S(1)}, f32[64]{0:T(128)S(1)}, u32[]{:S(2)}, u32[]{:S(2)}) collective-permute-start(f32[64]{0:T(128)S(1)} %maximum_bitcast_fusion), channel_id=1, source_target_pairs={{0,129},{128,0},{1,128},{129,1},{2,131},{130,2},{3,130},{131,3},{4... | collective-permute-start | bytes 776 | tf_op jit(solution)/shard_map/ppermute | solution.py:29
  32.5 18.7 %collective-permute-start.7 = (f32[64]{0:T(128)S(1)}, f32[64]{0:T(128)}, u32[]{:S(2)}, u32[]{:S(2)}) collective-permute-start(f32[64]{0:T(128)S(1)} %maximum_bitcast_fusion), channel_id=1, source_target_pairs={{0,1},{128,129},{1,0},{129,128},{2,3},{130,131},{3,2},{131,130},{4... | collective-permute-start | bytes 776 | tf_op jit(solution)/shard_map/ppermute | solution.py:29
  33.5 19.8 %collective-permute-start.6 = (f32[64]{0:T(128)S(1)}, f32[64]{0:T(128)S(1)}, u32[]{:S(2)}, u32[]{:S(2)}) collective-permute-start(f32[64]{0:T(128)S(1)} %maximum_bitcast_fusion), channel_id=1, source_target_pairs={{0,128},{128,1},{1,129},{129,0},{2,130},{130,3},{3,131},{131,2},{4... | collective-permute-start | bytes 776 | tf_op jit(solution)/shard_map/ppermute | solution.py:29
  48.5 21.8 %collective-permute-start.4 = (bf16[256,1792]{1,0:T(8,128)(2,1)}, bf16[256,1792]{1,0:T(8,128)(2,1)}, u32[]{:S(2)}, u32[]{:S(2)}) collective-permute-start(bf16[256,1792]{1,0:T(8,128)(2,1)} %get-tuple-element.70), channel_id=1, source_target_pairs={{0,1},{128,129},{1,0},{129,128},{2,3},{130,131},{3,2},{131,130},{4... | collective-permute-start | bytes 2752520 | tf_op jit(solution)/shard_map/ppermute | solution.py:29
  51.2 5.4 %collective-permute-start.5 = (bf16[128,640]{0,1:T(8,128)(2,1)}, bf16[128,640]{0,1:T(8,128)(2,1)S(1)}, u32[]{:S(2)}, u32[]{:S(2)}) collective-permute-start(bf16[128,640]{0,1:T(8,128)(2,1)} %pad_maximum_fusion.1), channel_id=1, source_target_pairs={{0,2},{2,0},{4,6},{6,4},{8,10},{10,8},{12,14},{14,12},{16,18},{18,... | collective-permute-start | bytes 491528 | tf_op jit(solution)/shard_map/ppermute | solution.py:33
  73.2 20.8 %collective-permute-start.9 = (bf16[256,1792]{1,0:T(8,128)(2,1)}, bf16[256,1792]{1,0:T(8,128)(2,1)}, u32[]{:S(2)}, u32[]{:S(2)}) collective-permute-start(bf16[256,1792]{1,0:T(8,128)(2,1)} %get-tuple-element.75.own), channel_id=1, source_target_pairs={{0,128},{128,1},{1,129},{129,0},{2,130},{130,3},{3,131},{131,2},{4... | collective-permute-start | bytes 2752520 | tf_op jit(solution)/shard_map/ppermute | solution.py:29
  74.5 19.5 %collective-permute-start.10 = (bf16[256,1792]{1,0:T(8,128)(2,1)}, bf16[256,1792]{1,0:T(8,128)(2,1)}, u32[]{:S(2)}, u32[]{:S(2)}) collective-permute-start(bf16[256,1792]{1,0:T(8,128)(2,1)} %get-tuple-element.75.own), channel_id=1, source_target_pairs={{0,129},{128,0},{1,128},{129,1},{2,131},{130,2},{3,130},{131,3},{4... | collective-permute-start | bytes 2752520 | tf_op jit(solution)/shard_map/ppermute | solution.py:29
  78.2 26.1 %all-to-all-start.1 = ((bf16[32,8,640]{2,1,0:T(8,128)(2,1)}), bf16[32,8,640]{2,1,0:T(8,128)(2,1)S(1)}, u32[]{:S(2)}, u32[]{:S(2)}) async-start(bf16[32,8,640]{2,1,0:T(8,128)(2,1)} %bitcast.24), calls=%async_computation.1 | async-start | bytes 655360 | tf_op jit(solution)/shard_map/all_to_all | solution.py:39
  94.0 43.8 %collective-permute-start.16 = (bf16[256,1792]{1,0:T(8,128)(2,1)}, bf16[256,1792]{1,0:T(8,128)(2,1)}, u32[]{:S(2)}, u32[]{:S(2)}) collective-permute-start(bf16[256,1792]{1,0:T(8,128)(2,1)} %get-tuple-element.47.own), channel_id=1, source_target_pairs={{0,128},{128,1},{1,129},{129,0},{2,130},{130,3},{3,131},{131,2},{4... | collective-permute-start | bytes 2752520 | tf_op jit(solution)/shard_map/ppermute | solution.py:29
  94.6 43.2 %collective-permute-start.17 = (bf16[256,1792]{1,0:T(8,128)(2,1)}, bf16[256,1792]{1,0:T(8,128)(2,1)}, u32[]{:S(2)}, u32[]{:S(2)}) collective-permute-start(bf16[256,1792]{1,0:T(8,128)(2,1)} %get-tuple-element.47.own), channel_id=1, source_target_pairs={{0,129},{128,0},{1,128},{129,1},{2,131},{130,2},{3,130},{131,3},{4... | collective-permute-start | bytes 2752520 | tf_op jit(solution)/shard_map/ppermute | solution.py:29
  98.5 25.1 %collective-permute-start.11 = (bf16[128,1792]{1,0:T(8,128)(2,1)}, bf16[128,1792]{1,0:T(8,128)(2,1)}, u32[]{:S(2)}, u32[]{:S(2)}) collective-permute-start(bf16[128,1792]{1,0:T(8,128)(2,1)} %slice.76), channel_id=1, source_target_pairs={{0,128},{128,1},{1,129},{129,0},{2,130},{130,3},{3,131},{131,2},{4... | collective-permute-start | bytes 1376264 | tf_op jit(solution)/shard_map/ppermute | solution.py:29
  100.3 23.3 %collective-permute-start.12 = (bf16[128,1792]{1,0:T(8,128)(2,1)}, bf16[128,1792]{1,0:T(8,128)(2,1)}, u32[]{:S(2)}, u32[]{:S(2)}) collective-permute-start(bf16[128,1792]{1,0:T(8,128)(2,1)} %slice.77), channel_id=1, source_target_pairs={{0,129},{128,0},{1,128},{129,1},{2,131},{130,2},{3,130},{131,3},{4... | collective-permute-start | bytes 1376264 | tf_op jit(solution)/shard_map/ppermute | solution.py:29
  128.2 5.3 %collective-permute-start.15 = (bf16[256,256]{1,0:T(8,128)(2,1)S(1)}, bf16[256,256]{1,0:T(8,128)(2,1)S(1)}, u32[]{:S(2)}, u32[]{:S(2)}) collective-permute-start(bf16[256,256]{1,0:T(8,128)(2,1)S(1)} %hidden_units.2.refs_0_), channel_id=1, source_target_pairs={{0,1},{128,129},{1,0},{129,128},{2,3},{130,131},{3,2},{131,130},{4... | collective-permute-start | bytes 393224 | tf_op jit(solution)/shard_map/ppermute | solution.py:29
  137.8 43.1 %all-to-all-start.3 = ((bf16[32,8,1792]{2,1,0:T(8,128)(2,1)}), bf16[32,8,1792]{2,1,0:T(8,128)(2,1)}, u32[]{:S(2)}, u32[]{:S(2)}) async-start(bf16[32,8,1792]{2,1,0:T(8,128)(2,1)} %bitcast.90), calls=%async_computation.3 | async-start | bytes 1835008 | tf_op jit(solution)/shard_map/all_to_all | solution.py:39
  152.2 14.3 %collective-permute-start.18 = (bf16[128,1792]{1,0:T(8,128)(2,1)}, bf16[128,1792]{1,0:T(8,128)(2,1)}, u32[]{:S(2)}, u32[]{:S(2)}) collective-permute-start(bf16[128,1792]{1,0:T(8,128)(2,1)} %slice.79), channel_id=1, source_target_pairs={{0,128},{128,1},{1,129},{129,0},{2,130},{130,3},{3,131},{131,2},{4... | collective-permute-start | bytes 1376264 | tf_op jit(solution)/shard_map/ppermute | solution.py:29
  154.2 12.3 %collective-permute-start.19 = (bf16[128,1792]{1,0:T(8,128)(2,1)}, bf16[128,1792]{1,0:T(8,128)(2,1)}, u32[]{:S(2)}, u32[]{:S(2)}) collective-permute-start(bf16[128,1792]{1,0:T(8,128)(2,1)} %slice.80), channel_id=1, source_target_pairs={{0,129},{128,0},{1,128},{129,1},{2,131},{130,2},{3,130},{131,3},{4... | collective-permute-start | bytes 1376264 | tf_op jit(solution)/shard_map/ppermute | solution.py:29
  168.6 6.0 %collective-permute-start.21 = (bf16[256,256]{1,0:T(8,128)(2,1)S(1)}, bf16[256,256]{1,0:T(8,128)(2,1)S(1)}, u32[]{:S(2)}, u32[]{:S(2)}) collective-permute-start(bf16[256,256]{1,0:T(8,128)(2,1)S(1)} %hidden_units.3.refs_0_), channel_id=1, source_target_pairs={{0,129},{128,0},{1,128},{129,1},{2,131},{130,2},{3,130},{131,3},{4... | collective-permute-start | bytes 393224 | tf_op jit(solution)/shard_map/ppermute | solution.py:29
  171.2 5.3 %collective-permute-start.22 = (bf16[256,256]{1,0:T(8,128)(2,1)S(1)}, bf16[256,256]{1,0:T(8,128)(2,1)S(1)}, u32[]{:S(2)}, u32[]{:S(2)}) collective-permute-start(bf16[256,256]{1,0:T(8,128)(2,1)S(1)} %hidden_units.3.refs_0_), channel_id=1, source_target_pairs={{0,1},{128,129},{1,0},{129,128},{2,3},{130,131},{3,2},{131,130},{4... | collective-permute-start | bytes 393224 | tf_op jit(solution)/shard_map/ppermute | solution.py:29
  180.9 25.4 %all-to-all-start.2 = ((bf16[32,8,1792]{2,1,0:T(8,128)(2,1)}), bf16[32,8,1792]{2,1,0:T(8,128)(2,1)S(1)}, u32[]{:S(2)}, u32[]{:S(2)}) async-start(bf16[32,8,1792]{2,1,0:T(8,128)(2,1)} %bitcast.28), calls=%async_computation.2 | async-start | bytes 1835008 | tf_op jit(solution)/shard_map/all_to_all | solution.py:39
  206.9 12.1 %collective-permute-start.23 = (bf16[32,1792]{1,0:T(8,128)(2,1)S(1)}, bf16[32,1792]{1,0:T(8,128)(2,1)S(1)}, u32[]{:S(2)}, u32[]{:S(2)}) collective-permute-start(bf16[32,1792]{1,0:T(8,128)(2,1)S(1)} %slice.128), channel_id=1, source_target_pairs={{0,2},{2,0},{4,6},{6,4},{8,10},{10,8},{12,14},{14,12},{16,18},{18,... | collective-permute-start | bytes 344072 | tf_op jit(solution)/shard_map/ppermute | solution.py:33
  (66 other events, 687.5 us)
